TPU v7x, 32 devices: a whole 2x2x4 slice. The times are simulated.
32 devices in a mesh: slab: 4 (over z), piece: 8 (over y, x, core).
Axes of the slice: x: 2, y: 2, z: 4, core: 2. Of those that a mesh axis runs over, the one named last changes fastest.
Arguments:
- fine_tiles: bfloat16 [256, 64, 512], P(('slab', 'piece')), may hold values from -0.25 to 0.25
- fine_cols: int32 [256, 8], P(('slab', 'piece')), may hold values from 0 to 23
- bond_mask: int32 [256, 8], P(('slab', 'piece')), may hold values 0 or 1
- diag_inv: bfloat16 [256, 64, 64], P(('slab', 'piece')), may hold values from -0.75 to 0.75
- tentative: bfloat16 [256, 64, 64], P(('slab', 'piece')), may hold values from -0.75 to 0.75
- aggregate: int32 [256], P(('slab', 'piece')), may hold values from 0 to 7
- tentative_two: bfloat16 [256, 64, 64], P(('slab', 'piece')), may hold values from -0.75 to 0.75
- aggregate_two: int32 [256], P(('slab', 'piece')), may hold values from 0 to 7
Outputs:
- coarse_one: float32 [256, 64, 3584], P(('slab', 'piece'))
- coarse_two: float32 [32, 64, 3584], P(('slab', 'piece'))
All inputs are finite; a program needn't handle non-finite values. No bound on the sum of `bond_mask` on one device may be relied on, other than what follows from the above.
Results may differ from a plain program's by a relative error of at most 0.008.
Values may be sent and summed in bfloat16 or wider, within the bound.
A program may use at most 128 MiB of HBM per device.

v0:
```python
import jax
import jax.numpy as jnp
from jax import lax
from jax.sharding import PartitionSpec as P

DAMPING = 2.0 / 3.0
EXACT_MODE = lax.Precision.HIGHEST


def padded_2(cells, sides, width):
    for axis, dim in sides:
        count = lax.axis_size(axis)
        ends = count - 1
        head = lax.slice_in_dim(cells, 0, width, axis=dim)
        tail = lax.slice_in_dim(cells, cells.shape[dim] - width, cells.shape[dim], axis=dim)
        cells = jnp.concatenate(
            [
                lax.ppermute(tail, axis, [(i, (i + 1) % count) for i in range(ends)]),
                cells,
                lax.ppermute(head, axis, [((i + 1) % count, i) for i in range(ends)]),
            ],
            axis=dim,
        )
    return cells


def passed_along(block, axis, distance):
    devices = range(lax.axis_size(axis))
    route = [(i - distance, i) for i in devices if i - distance in devices]
    return lax.ppermute(block, axis, route)


def slot_tiles(tiles, agg_ids, count):
    onehot = (agg_ids[:, None] == jnp.arange(count, dtype=jnp.int32)[None, :]).astype(jnp.float32)
    placed = tiles.astype(jnp.float32)[:, :, None, :] * onehot[:, None, :, None]
    return placed.astype(jnp.bfloat16).reshape(
        tiles.shape[0], tiles.shape[1], count * tiles.shape[2]
    )


def prolong_rows(quad, fine_cols, bond_mask, diag_inv, own_slot, basis_rim):
    blocks, tile_size = (diag_inv.shape[0], diag_inv.shape[1])
    slot_count = fine_cols.shape[1]
    agg_width = own_slot.shape[2]
    smooth = jnp.einsum("irs,iskt->ikrt", diag_inv, quad, preferred_element_type=jnp.float32)
    smooth = (DAMPING * bond_mask.astype(jnp.float32)[:, :, None, None] * smooth).astype(
        jnp.bfloat16
    )
    summed = jnp.zeros((blocks, tile_size, 3, agg_width), jnp.float32)
    for k in range(slot_count):
        column = fine_cols[:, k]
        rows_in = jnp.take(basis_rim, column, axis=0)
        product = jnp.einsum(
            "irs,isq->irq", smooth[:, k], rows_in, preferred_element_type=jnp.float32
        )
        side_mask = (column[:, None] // blocks == jnp.arange(3, dtype=jnp.int32)[None, :]).astype(
            jnp.float32
        )
        summed = summed - product[:, :, None, :] * side_mask[:, None, :, None]
    summed = summed.at[:, :, 1, :].add(own_slot.astype(jnp.float32))
    return summed.reshape(blocks, tile_size, 3 * agg_width).astype(jnp.bfloat16)


def apply_rows(quad, fine_cols, bond_mask, prolong_rim, agg_width):
    blocks, tile_size = (quad.shape[0], quad.shape[1])
    slot_count = fine_cols.shape[1]
    masked = quad * bond_mask.astype(jnp.bfloat16)[:, None, :, None]
    sides = jnp.zeros((blocks, tile_size, 3, 3 * agg_width), jnp.float32)
    for k in range(slot_count):
        column = fine_cols[:, k]
        rows_in = jnp.take(prolong_rim, column, axis=0)
        product = jnp.einsum(
            "irs,isq->irq", masked[:, :, k, :], rows_in, preferred_element_type=jnp.float32
        )
        side_mask = (column[:, None] // blocks == jnp.arange(3, dtype=jnp.int32)[None, :]).astype(
            jnp.float32
        )
        sides = sides + product[:, :, None, :] * side_mask[:, None, :, None]
    summed = jnp.pad(sides[:, :, 0], ((0, 0), (0, 0), (0, 2 * agg_width)))
    summed = summed + jnp.pad(sides[:, :, 1], ((0, 0), (0, 0), (agg_width, agg_width)))
    summed = summed + jnp.pad(sides[:, :, 2], ((0, 0), (0, 0), (2 * agg_width, 0)))
    return summed.astype(jnp.bfloat16)


def level_partial(coarse_rows, two_tiles, two_ids, basis, groups):
    agg_count, tile_size = (two_tiles.shape[0], two_tiles.shape[1])
    left = jnp.einsum(
        "ars,arc->asc", two_tiles.astype(jnp.float32), coarse_rows, precision=EXACT_MODE
    )
    left = left.reshape(agg_count, tile_size, 7, agg_count, tile_size)
    right = basis.astype(jnp.float32).reshape(7, agg_count, tile_size, groups * tile_size)
    both = jnp.einsum("asobt,obtq->asoq", left, right, precision=EXACT_MODE)
    onehot = (two_ids[:, None] == jnp.arange(groups, dtype=jnp.int32)[None, :]).astype(jnp.float32)
    placed = jnp.einsum("ag,asoq->gsoq", onehot, both, precision=EXACT_MODE)
    return placed.reshape(groups, tile_size, 7 * groups * tile_size)


def per_device(
    fine_tiles, fine_cols, bond_mask, diag_inv, tentative, aggregate, tentative_two, aggregate_two
):
    blocks, tile_size = (diag_inv.shape[0], diag_inv.shape[1])
    slot_count = fine_cols.shape[1]
    agg_count = tentative_two.shape[0]
    groups = lax.axis_size("piece")
    agg_width = agg_count * tile_size
    quad = fine_tiles.reshape(blocks, tile_size, slot_count, tile_size)
    qslot = slot_tiles(tentative, aggregate, agg_count)
    basis_rim = padded_2(qslot, (("slab", 0),), blocks)
    prolong = prolong_rows(quad, fine_cols, bond_mask, diag_inv, qslot, basis_rim)
    prolong_rim = padded_2(prolong, (("slab", 0),), blocks)
    applied = apply_rows(quad, fine_cols, bond_mask, prolong_rim, agg_width)
    product = lax.dot_general(
        prolong.reshape(blocks * tile_size, 3 * agg_width),
        applied.reshape(blocks * tile_size, 5 * agg_width),
        (((0,), (0,)), ((), ())),
        preferred_element_type=jnp.float32,
    )
    row_parts = product.reshape(3, agg_count, tile_size, 5 * agg_width)
    from_next = passed_along(row_parts[0].astype(jnp.bfloat16), "slab", -1).astype(jnp.float32)
    from_prev = passed_along(row_parts[2].astype(jnp.bfloat16), "slab", 1).astype(jnp.float32)
    coarse = jnp.pad(row_parts[1], ((0, 0), (0, 0), (agg_width, agg_width)))
    coarse = coarse + jnp.pad(from_next, ((0, 0), (0, 0), (2 * agg_width, 0)))
    coarse = coarse + jnp.pad(from_prev, ((0, 0), (0, 0), (0, 2 * agg_width)))
    q2slot = slot_tiles(tentative_two, aggregate_two, groups)
    gathered = lax.all_gather(q2slot, "slab", axis=0, tiled=True)
    padded = jnp.pad(gathered, ((3 * agg_count, 3 * agg_count), (0, 0), (0, 0)))
    basis = lax.dynamic_slice_in_dim(padded, lax.axis_index("slab") * agg_count, 7 * agg_count, 0)
    partial_value = level_partial(coarse, tentative_two, aggregate_two, basis, groups)
    summed = lax.psum(partial_value.astype(jnp.bfloat16), "piece").astype(jnp.float32)
    level_two = lax.dynamic_slice_in_dim(summed, lax.axis_index("piece"), 1, 0)
    return (coarse, level_two)


def solution(mesh):
    placed = (
        P(("slab", "piece"), None, None),
        P(("slab", "piece"), None),
        P(("slab", "piece"), None),
        P(("slab", "piece"), None, None),
        P(("slab", "piece"), None, None),
        P(("slab", "piece")),
        P(("slab", "piece"), None, None),
        P(("slab", "piece")),
    )
    return jax.shard_map(
        per_device,
        mesh=mesh,
        in_specs=placed,
        out_specs=(P(("slab", "piece"), None, None), P(("slab", "piece"), None, None)),
        check_vma=False,
    )
```

profile of v0, /device:TPU:0, one launch (start us, length us, event | category | flops | bytes accessed | tf_op | source)
XLA Modules:
  0.0 431.0 jit_solution(3605054724448161543)
XLA Ops:
  10.0 5.7 %collective-permute-start = (bf16[8,64,512]{2,1,0:T(8,128)(2,1)}, bf16[8,64,512]{2,1,0:T(8,128)(2,1)}, u32[]{:S(2)}, u32[]{:S(2)}) collective-permute-start(bf16[8,64,512]{2,1,0:T(8,128)(2,1)} %multiply_convert_fusion.2), channel_id=1, source_target_pairs={{0,8},{8,16},{16,24},{1,9},{9,17},{17,25},{2,10},{10,18},{18,26},{... | collective-permute-start | bytes 1572872 | tf_op jit(solution)/shard_map/ppermute | solution.py:18
  26.4 4.9 %collective-permute-done.1 = bf16[8,64,512]{2,1,0:T(8,128)(2,1)} collective-permute-done((bf16[8,64,512]{2,1,0:T(8,128)(2,1)}, bf16[8,64,512]{2,1,0:T(8,128)(2,1)}, u32[]{:S(2)}, u32[]{:S(2)}) %collective-permute-start.1) | collective-permute-done | bytes 524320 | tf_op jit(solution)/shard_map/ppermute | solution.py:20
  48.5 5.0 %multiply_subtract_fusion = f32[8,64,3,512]{3,2,1,0:T(4,128)S(1)} fusion(f32[8,3]{1,0:T(8,128)S(1)} %get-tuple-element.46, f32[8,64,512]{2,1,0:T(8,128)S(1)} %fusion.41, f32[8,3]{1,0:T(8,128)S(1)} %get-tuple-element.45, f32[8,64,512]{2,1,0:T(8,128)S(1)} %fusion.43, f32[8,3]{1,0:T(8,128)S(1)} %get-tuple-element.44, f32[8,64,512]{2,1,0:T(8,128)S(1)} %fusion.45, ...), kind=kLoop, calls=%fused_computation.26 | loop fusion | flops 12582912 | bytes 11535104 | tf_op jit(solution)/shard_map/sub | solution.py:59
  57.2 21.0 %scatter-add.4 = f32[8,64,3,512]{3,2,1,0:T(4,128)} dynamic-update-slice(f32[8,64,3,512]{3,2,1,0:T(4,128)} %copy-done.3, f32[8,64,1,512]{3,2,1,0:T(1,128)S(1)} %slice_add_fusion, s32[]{:T(128)} %constant.139.clone.1, s32[]{:T(128)} %constant.139.clone.1, s32[]{:T(128)} %constant.138.clone.1, s32[]{:T(128)} %constant.139.clone.1) | dynamic-update-slice | bytes 2097156 | tf_op jit(solution)/shard_map/scatter-add | solution.py:60
  84.2 4.0 collective-permute-start.2
  95.7 43.4 %collective-permute-done.2 = bf16[8,64,1536]{2,1,0:T(8,128)(2,1)} collective-permute-done((bf16[8,64,1536]{2,1,0:T(8,128)(2,1)}, bf16[8,64,1536]{2,1,0:T(8,128)(2,1)}, u32[]{:S(2)}, u32[]{:S(2)}) %collective-permute-start.2) | collective-permute-done | bytes 1572896 | tf_op jit(solution)/shard_map/ppermute | solution.py:18
  143.1 15.7 %collective-permute-done.3 = bf16[8,64,1536]{2,1,0:T(8,128)(2,1)} collective-permute-done((bf16[8,64,1536]{2,1,0:T(8,128)(2,1)}, bf16[8,64,1536]{2,1,0:T(8,128)(2,1)}, u32[]{:S(2)}, u32[]{:S(2)}) %collective-permute-start.3) | collective-permute-done | bytes 1572896 | tf_op jit(solution)/shard_map/ppermute | solution.py:20
  161.4 4.1 gather_fusion.13
  165.6 4.2 gather_fusion.12
  169.7 4.2 gather_fusion.11
  174.0 4.2 gather_fusion.10
  184.1 4.1 gather_fusion.14
  188.2 4.1 gather_fusion.15
  203.8 6.2 %multiply_add_fusion = f32[8,64,3,1536]{3,1,0,2:T(8,128)S(1)} fusion(f32[8,3]{0,1:T(4,128)S(1)} %copy.70, f32[8,64,1536]{2,1,0:T(8,128)} %fusion.7, f32[8,3]{0,1:T(4,128)S(1)} %copy.69, f32[8,64,1536]{2,1,0:T(8,128)S(1)} %fusion.9, f32[8,3]{0,1:T(4,128)S(1)} %copy.68, f32[8,64,1536]{2,1,0:T(8,128)S(1)} %fusion.11, f32[8,3]{0,1:T(4,128)S(1)} %copy.67, ...), kind=kLoop, calls=%fused_computation.19 | loop fusion | flops 35389440 | bytes 34603776 | tf_op jit(solution)/shard_map/add | solution.py:78
  214.0 11.5 %fusion.129 = (bf16[1536,2560]{1,0:T(8,128)(2,1)S(1)}, f32[1536,2560]{1,0:T(8,128)}) fusion(bf16[8,64,1536]{2,1,0:T(8,128)(2,1)S(1)} %copy-done.6, f32[8,64,1536]{2,1,0:T(8,128)} %get-tuple-element.33, f32[8,64,1536]{2,1,0:T(8,128)} %get-tuple-element.34, f32[8,64,1536]{2,1,0:T(8,128)} %get-tuple-element.32), kind=kOutput, calls=%fused_computation.261 | convolution fusion | flops 4034396160 | bytes 34603008 | tf_op jit(solution)/shard_map/dot_general | solution.py:112
  229.4 6.1 %collective-permute-start.5 = (bf16[8,64,2560]{2,1,0:T(8,128)(2,1)}, bf16[8,64,2560]{2,1,0:T(8,128)(2,1)}, u32[]{:S(2)}, u32[]{:S(2)}) collective-permute-start(bf16[8,64,2560]{2,1,0:T(8,128)(2,1)} %bitcast.25), channel_id=1, source_target_pairs={{0,8},{8,16},{16,24},{1,9},{9,17},{17,25},{2,10},{10,18},{18,26},{... | collective-permute-start | bytes 7864328 | tf_op jit(solution)/shard_map/ppermute | solution.py:30
  235.5 5.2 %slice.213 = f32[512,2560]{1,0:T(8,128)} slice(f32[1536,2560]{1,0:T(8,128)} %get-tuple-element.38), slice={[512:1024], [0:2560]} | slice | bytes 10485760 | tf_op jit(solution)/shard_map/slice | solution.py:121
  240.7 4.7 %pad_dynamic-slice_fusion = bf16[56,64,512]{2,1,0:T(8,128)(2,1)} fusion(s32[]{:T(128)S(6)} %select_n.61, bf16[32,64,512]{2,1,0:T(8,128)(2,1)} %all-gather.2.cloned.1.call-done), kind=kLoop, calls=%fused_computation.24 | loop fusion | bytes 5767172 | tf_op jit(solution)/shard_map/dynamic_slice | solution.py:127
  245.4 41.0 %collective-permute-done.4 = bf16[8,64,2560]{2,1,0:T(8,128)(2,1)S(1)} collective-permute-done((bf16[8,64,2560]{2,1,0:T(8,128)(2,1)}, bf16[8,64,2560]{2,1,0:T(8,128)(2,1)S(1)}, u32[]{:S(2)}, u32[]{:S(2)}) %collective-permute-start.4) | collective-permute-done | bytes 2621472 | tf_op jit(solution)/shard_map/ppermute | solution.py:30
  293.3 5.9 %convolution_bitcast_fusion.1 = f32[8,64,3584]{2,1,0:T(8,128)} fusion(f32[8,64,3584]{2,1,0:T(8,128)S(1)} %convert_add_fusion, bf16[8,64,64]{2,1,0:T(8,128)(2,1)S(1)} %copy-done.21), kind=kOutput, calls=%fused_computation.23 | convolution fusion | flops 1409286144 | bytes 14745600 | tf_op jit(solution)/shard_map/ars,arc->asc/dot_general | solution.py:87
  299.2 11.3 %reshape.330 = f32[8,64,7,8,64]{4,3,2,1,0:T(8,128)} reshape(f32[8,64,3584]{2,1,0:T(8,128)} %convolution_bitcast_fusion.1) | data formatting | bytes 14680064 | tf_op jit(solution)/shard_map/reshape | solution.py:90
  310.5 20.7 %fusion = f32[7,512,8,64,1]{1,2,4,0,3:T(8,128)S(1)} fusion(bf16[7,8,64,512,1]{3,2,1,0,4:T(8,128)(2,1)} %bitcast.95, f32[8,64,7,8,64]{4,3,2,1,0:T(8,128)} %reshape.330), kind=kOutput, calls=%fused_computation.16 | convolution fusion | flops 11274289152 | bytes 18350080 | tf_op jit(solution)/shard_map/asobt,obtq->asoq/dot_general | solution.py:92
  338.3 8.3 %convert_element_type.190 = bf16[8,64,3584]{2,1,0:T(8,128)(2,1)} reshape(bf16[8,64,7,512]{3,2,1,0:T(8,128)(2,1)} %copy.74) | data formatting | bytes 7340032 | tf_op jit(solution)/shard_map/convert_element_type | solution.py:129
  346.6 75.5 %all-reduce.9.cloned.1.call-done = bf16[8,64,3584]{2,1,0:T(8,128)(2,1)} async-done(((bf16[8,64,3584]{2,1,0:T(8,128)(2,1)}), bf16[8,64,3584]{2,1,0:T(8,128)(2,1)}) %all-reduce.9.cloned.1.call-update) | async-done | bytes 3670032 | tf_op jit(solution)/shard_map/psum | solution.py:129
  (150 shorter events, 95.2 us)
Async XLA Ops:
  7.2 13.8 %copy-start = (bf16[8,64,64]{2,1,0:T(8,128)(2,1)S(1)}, bf16[8,64,64]{2,1,0:T(8,128)(2,1)}, u32[]{:S(2)}) copy-start(bf16[8,64,64]{2,1,0:T(8,128)(2,1)} %param.17) | copy-start | bytes 196612
  7.2 9.8 %copy-start.22 = (s32[8,8]{1,0:T(8,128)S(1)}, s32[8,8]{1,0:T(8,128)}, u32[]{:S(2)}) copy-start(s32[8,8]{1,0:T(8,128)} %param.15) | copy-start | bytes 772
  7.2 10.3 %copy-start.23 = (s32[8,8]{1,0:T(8,128)S(1)}, s32[8,8]{1,0:T(8,128)}, u32[]{:S(2)}) copy-start(s32[8,8]{1,0:T(8,128)} %param.16) | copy-start | bytes 772
  7.2 233.5 %all-gather.2.cloned.1.call-start = ((), (), s32[]{:S(2)}) async-start(), calls=%async_computation | async-start | bytes 2621440 | tf_op jit(solution)/shard_map/all_gather | solution.py:125
  10.0 16.4 %collective-permute-start = (bf16[8,64,512]{2,1,0:T(8,128)(2,1)}, bf16[8,64,512]{2,1,0:T(8,128)(2,1)}, u32[]{:S(2)}, u32[]{:S(2)}) collective-permute-start(bf16[8,64,512]{2,1,0:T(8,128)(2,1)} %multiply_convert_fusion.2), channel_id=1, source_target_pairs={{0,8},{8,16},{16,24},{1,9},{9,17},{17,25},{2,10},{10,18},{18,26},{... | collective-permute-start | bytes 1572872 | tf_op jit(solution)/shard_map/ppermute | solution.py:18
  15.7 15.6 %collective-permute-start.1 = (bf16[8,64,512]{2,1,0:T(8,128)(2,1)}, bf16[8,64,512]{2,1,0:T(8,128)(2,1)}, u32[]{:S(2)}, u32[]{:S(2)}) collective-permute-start(bf16[8,64,512]{2,1,0:T(8,128)(2,1)} %multiply_convert_fusion.2), channel_id=1, source_target_pairs={{8,0},{16,8},{24,16},{9,1},{17,9},{25,17},{10,2},{18,10},{26,18},{... | collective-permute-start | bytes 1572872 | tf_op jit(solution)/shard_map/ppermute | solution.py:20
  20.8 5.6 %copy-start.13 = (bf16[8,64,8,64]{3,2,1,0:T(8,128)(2,1)}, bf16[8,64,8,64]{3,2,1,0:T(8,128)(2,1)S(1)}, u32[]{:S(2)}) copy-start(bf16[8,64,8,64]{3,2,1,0:T(8,128)(2,1)S(1)} %reshape.328) | copy-start | bytes 1572868
  43.0 3.2 copy-start.19
  43.0 3.2 copy-start.20
  43.0 3.6 copy-start.18
  43.1 3.9 copy-start.17
  81.1 8.6 %copy-start.21 = (bf16[8,64,64]{2,1,0:T(8,128)(2,1)S(1)}, bf16[8,64,64]{2,1,0:T(8,128)(2,1)}, u32[]{:S(2)}) copy-start(bf16[8,64,64]{2,1,0:T(8,128)(2,1)} %param.20) | copy-start | bytes 196612
  84.2 7.1 %copy-start.24 = (s32[8]{0:T(128)S(1)}, s32[8]{0:T(128)}, u32[]{:S(2)}) copy-start(s32[8]{0:T(128)} %param.21) | copy-start | bytes 100
  84.2 54.9 %collective-permute-start.2 = (bf16[8,64,1536]{2,1,0:T(8,128)(2,1)}, bf16[8,64,1536]{2,1,0:T(8,128)(2,1)}, u32[]{:S(2)}, u32[]{:S(2)}) collective-permute-start(bf16[8,64,1536]{2,1,0:T(8,128)(2,1)} %convert_element_type.181), channel_id=1, source_target_pairs={{0,8},{8,16},{16,24},{1,9},{9,17},{17,25},{2,10},{10,18},{18,26},{... | collective-permute-start | bytes 4718600 | tf_op jit(solution)/shard_map/ppermute | solution.py:18
  88.2 70.6 %collective-permute-start.3 = (bf16[8,64,1536]{2,1,0:T(8,128)(2,1)}, bf16[8,64,1536]{2,1,0:T(8,128)(2,1)}, u32[]{:S(2)}, u32[]{:S(2)}) collective-permute-start(bf16[8,64,1536]{2,1,0:T(8,128)(2,1)} %convert_element_type.181), channel_id=1, source_target_pairs={{8,0},{16,8},{24,16},{9,1},{17,9},{25,17},{10,2},{18,10},{26,18},{... | collective-permute-start | bytes 4718600 | tf_op jit(solution)/shard_map/ppermute | solution.py:20
  89.8 4.7 %copy-start.14 = (bf16[8,64,8,64]{3,2,1,0:T(8,128)(2,1)S(1)}, bf16[8,64,8,64]{3,2,1,0:T(8,128)(2,1)}, u32[]{:S(2)}) copy-start(bf16[8,64,8,64]{3,2,1,0:T(8,128)(2,1)} %copy-done.13) | copy-start | bytes 1572868
  93.7 48.1 %copy-start.5 = (bf16[8,64,1536]{2,1,0:T(8,128)(2,1)S(1)}, bf16[8,64,1536]{2,1,0:T(8,128)(2,1)}, u32[]{:S(2)}) copy-start(bf16[8,64,1536]{2,1,0:T(8,128)(2,1)} %convert_element_type.181) | copy-start | bytes 4718596
  93.7 328.4 %all-reduce.9.cloned.1.call-start = ((), (), s32[]{:S(2)}) async-start(), calls=%async_computation.1 | async-start | bytes 7340032 | tf_op jit(solution)/shard_map/psum | solution.py:129
  210.0 4.0 copy-start.6
  228.1 58.3 %collective-permute-start.4 = (bf16[8,64,2560]{2,1,0:T(8,128)(2,1)}, bf16[8,64,2560]{2,1,0:T(8,128)(2,1)S(1)}, u32[]{:S(2)}, u32[]{:S(2)}) collective-permute-start(bf16[8,64,2560]{2,1,0:T(8,128)(2,1)} %bitcast.24), channel_id=1, source_target_pairs={{8,0},{16,8},{24,16},{9,1},{17,9},{25,17},{10,2},{18,10},{26,18},{... | collective-permute-start | bytes 7864328 | tf_op jit(solution)/shard_map/ppermute | solution.py:30
  229.4 58.3 %collective-permute-start.5 = (bf16[8,64,2560]{2,1,0:T(8,128)(2,1)}, bf16[8,64,2560]{2,1,0:T(8,128)(2,1)}, u32[]{:S(2)}, u32[]{:S(2)}) collective-permute-start(bf16[8,64,2560]{2,1,0:T(8,128)(2,1)} %bitcast.25), channel_id=1, source_target_pairs={{0,8},{8,16},{16,24},{1,9},{9,17},{17,25},{2,10},{10,18},{18,26},{... | collective-permute-start | bytes 7864328 | tf_op jit(solution)/shard_map/ppermute | solution.py:30
  240.7 47.0 %copy-start.4 = (f32[512,2560]{1,0:T(8,128)S(1)}, f32[512,2560]{1,0:T(8,128)}, u32[]{:S(2)}) copy-start(f32[512,2560]{1,0:T(8,128)} %slice.213) | copy-start | bytes 15728644
  290.2 3.1 copy-start.2
  338.3 85.8 %copy-start.1 = (bf16[8,64,64]{2,1,0:T(8,128)(2,1)S(1)}, bf16[8,64,64]{2,1,0:T(8,128)(2,1)}, u32[]{:S(2)}) copy-start(bf16[8,64,64]{2,1,0:T(8,128)(2,1)} %param.17) | copy-start | bytes 196612
  (10 other events, 18.0 us)
Sparse Core Ops, SparseCore 0:
  93.8 62.0 all-gather.1
  346.7 75.3 all-reduce.8
where the time goes:
time: 433 us; the launch traced here: 431 us
  waiting for transfers between devices  186 us (43%)
  local copies, waits for them, and re-layouts  127 us (29%)
  matrix products  56.7 us (13%)
  other arithmetic  27 us (6%)
  starting transfers between devices  19.9 us (5%)
  between operations  14.7 us (3%)
    psum x1, waiting for transfers between devices, per_device(): lax.psum(partial_value.astype(jnp.bfloat16), 'piece').astype(jnp.float32)  75.5 us
    ppermute x2, waiting for transfers between devices, padded_2(): lax.ppermute(tail, axis, [(i, (i + 1) % count) for i in range(ends)])  47.4 us
    ppermute x2, waiting for transfers between devices, passed_along(): return lax.ppermute(block, axis, route)  42.3 us
    gather x8, local copies, waits for them, and re-layouts, apply_rows(): rows_in = jnp.take(prolong_rim, column, axis=0)  30.9 us
    scatter-add x1, local copies, waits for them, and re-layouts, prolong_rows(): summed = summed.at[:, :, 1, :].add(own_slot.astype(jnp.float32))  21 us
    dot_general x1, matrix products, level_partial(): both = jnp.einsum('asobt,obtq->asoq', left, right, precision=EXACT_MODE)  20.7 us
    ppermute x2, waiting for transfers between devices, padded_2(): lax.ppermute(head, axis, [((i + 1) % count, i) for i in range(ends)])  20.6 us
    unnamed x54, local copies, waits for them, and re-layouts  12.2 us
  transfers between devices with their start and end apart: 8, of which 7 were waited for; matrix products, arithmetic and copies ran while one was open for 21% of the time, Pallas kernels for 0%

commit v1 on v0

v1 whole, which is shorter than its diff:
```python
import functools

import jax
import jax.numpy as jnp
from jax import lax
from jax.experimental import pallas as pl
from jax.experimental.pallas import tpu as pltpu
from jax.sharding import PartitionSpec as P

DAMPING = 2.0 / 3.0
LANES = 128
MESH = pl.DeviceIdType.MESH
VMEM_LIMIT = 56 * 1024 * 1024
F32 = jnp.float32
BF16 = jnp.bfloat16


def mm(a, b):
    return jnp.dot(a, b, preferred_element_type=F32)


def gather_kernel(n, far, a_ref, d_ref, t_ref, q_ref, i_ref, ag, dg, tg, ig, send_sem, recv_sem):
    s, p = lax.axis_index("slab"), lax.axis_index("piece")
    barrier = pltpu.get_barrier_semaphore()

    @pl.when(s > 0)
    def _():
        pl.semaphore_signal(barrier, inc=1, device_id=(s - 1, p), device_id_type=MESH)

    @pl.when(s < n - 1)
    def _():
        pl.semaphore_signal(barrier, inc=1, device_id=(s + 1, p), device_id_type=MESH)

    half = d_ref.shape[0] // 2
    ag[s] = a_ref[...]
    dg[s] = jnp.concatenate([d_ref[0:half, :], d_ref[half : 2 * half, :]], axis=1)
    tg[s] = jnp.concatenate([t_ref[...], q_ref[...]], axis=1)
    ig[s] = i_ref[...]

    peers = jnp.where(s > 0, 1, 0) + jnp.where(s < n - 1, 1, 0)
    pl.semaphore_wait(barrier, peers)

    arrays = (ig, tg, dg, ag)
    reach = (far, far, 2, 2)

    def copy(way, step, which, slab):
        there = s + 1 if way == 0 else s - 1
        return pltpu.make_async_remote_copy(
            src_ref=arrays[which].at[slab],
            dst_ref=arrays[which].at[slab],
            send_sem=send_sem.at[way, step, which],
            recv_sem=recv_sem.at[way, step, which],
            device_id=(there, p),
            device_id_type=MESH,
        )

    def sends(way, step):
        if way == 0:
            return (s - step >= 0) & (s + 1 < n), s - step
        return (s + step < n) & (s >= 1), s + step

    def gets(way, step):
        if way == 0:
            return s - 1 - step >= 0, s - 1 - step
        return s + 1 + step < n, s + 1 + step

    steps = min(far, n - 1)
    for step in range(steps + 1):
        for which in range(4):
            for way in range(2):
                if 0 < step <= min(reach[which], steps):
                    ok, slab = gets(way, step - 1)

                    @pl.when(ok)
                    def _(way=way, which=which, slab=slab):
                        copy(way, step - 1, which, slab).wait_recv()

                if step < min(reach[which], steps):
                    ok, slab = sends(way, step)

                    @pl.when(ok)
                    def _(way=way, which=which, slab=slab):
                        copy(way, step, which, slab).start()

    for step in range(steps):
        for which in range(4):
            for way in range(2):
                if step < reach[which]:
                    ok, slab = sends(way, step)

                    @pl.when(ok)
                    def _(way=way, which=which, slab=slab):
                        copy(way, step, which, slab).wait_send()


def level_kernel(
    n, blocks, slots, aggs, groups, tile, s_ref, i_ref, ag, dg, tg,
    out, cb, t2s, t2t, ad, sd, pro, ts, acc, bd, wm,
):
    s = s_ref[0]
    rows, w, gw = blocks * tile, aggs * tile, groups * tile
    pair = 2 * tile
    lane = lax.broadcasted_iota(jnp.int32, (tile, pair), 1) // tile

    for v in range(n):
        near = jnp.abs(v - s) <= 3
        for b in range(blocks):
            x = tg[v, b * tile : (b + 1) * tile, :].astype(F32)
            turned = pltpu.roll(x, tile, 1)
            one = jnp.where(lane == 0, x, turned)
            two = jnp.where(lane == 0, turned, x)
            g1 = jnp.where(near, i_ref[v, 2, b], -1)
            g2 = jnp.where(near, i_ref[v, 3, b], -1)
            for q in range(w // pair):
                ts[v, b * tile : (b + 1) * tile, q * pair : (q + 1) * pair] = jnp.where(
                    lane + 2 * q == g1, one, 0.0
                ).astype(BF16)
            for q in range(gw // pair):
                t2s[v, b * tile : (b + 1) * tile, q * pair : (q + 1) * pair] = jnp.where(
                    lane + 2 * q == g2, two, 0.0
                ).astype(BF16)

    t2t[...] = t2s[s].astype(F32).T.astype(BF16)
    bd[...] = jnp.zeros_like(bd)

    for e in range(-2, 3):
        u = s + e

        @pl.when((u >= 0) & (u < n))
        def _(e=e, u=u):
            def row(i, carry):
                acc[...] = jnp.zeros_like(acc)
                base = pl.multiple_of(i * tile, tile)
                for k2 in range(slots // 2):
                    x = ag[u, pl.ds(base, tile), k2 * pair : (k2 + 1) * pair].astype(F32)
                    turned = pltpu.roll(x, tile, 1)
                    for odd in range(2):
                        k = 2 * k2 + odd
                        c = i_ref[u, 0, i * slots + k]
                        m = i_ref[u, 1, i * slots + k]
                        side = lax.rem(c, 2)
                        y = jnp.where(side == odd, x, turned)
                        keep = jnp.where(m != 0, side, -1)
                        at = pl.multiple_of((c // 2) * pair, pair)
                        acc[:, pl.ds(at, pair)] += jnp.where(lane == keep, y, 0.0)
                ad[e + 2, pl.ds(base, tile), :] = acc[...].astype(BF16)
                return carry

            lax.fori_loop(0, blocks, row, 0)
            half = blocks // 2
            for h in range(2):
                for b in range(half):
                    x = dg[u, b * tile : (b + 1) * tile, :].astype(F32)
                    if b % 2 != h:
                        x = pltpu.roll(x, tile, 1)
                    bd[b * tile : (b + 1) * tile, (b // 2) * pair : (b // 2 + 1) * pair] = (
                        jnp.where(lane == b % 2, x, 0.0).astype(BF16)
                    )
                lo = h * half * tile
                hi = lo + half * tile
                sd[lo:hi, :] = (DAMPING * mm(bd[...], ad[e + 2, lo:hi, :])).astype(BF16)
            for j in range(3):
                v = u + j - 1
                inside = (v >= 0) & (v < n)

                @pl.when(inside)
                def _(j=j, v=v):
                    value = -mm(sd[:, j * rows : (j + 1) * rows], ts[v])
                    if j == 1:
                        value = value + ts[v].astype(F32)
                    pro[e + 2, :, j * w : (j + 1) * w] = value.astype(BF16)

                @pl.when(jnp.logical_not(inside))
                def _(j=j):
                    pro[e + 2, :, j * w : (j + 1) * w] = jnp.zeros((rows, w), BF16)

        @pl.when((u < 0) | (u >= n))
        def _(e=e):
            pro[e + 2] = jnp.zeros((rows, 3 * w), BF16)
            if abs(e) < 2:
                ad[e + 2] = jnp.zeros((rows, 3 * rows), BF16)

    turned = [pro[dj + 2, :, (1 - dj) * w : (2 - dj) * w].astype(F32).T.astype(BF16) for dj in (-1, 0, 1)]
    for e in range(-2, 3):
        total = None
        for dj in (-1, 0, 1):
            j = e - dj + 1
            if 0 <= j < 3:
                term = mm(turned[dj + 1], ad[dj + 2, :, j * rows : (j + 1) * rows])
                total = term if total is None else total + term
        wm[e + 2] = total.astype(BF16)

    short = n < 7
    for f in range(-3, 4):
        t = s + f
        inside = (t >= 0) & (t < n)

        @pl.when(inside)
        def _(f=f, t=t):
            total = None
            for e in range(max(-2, f - 1), min(2, f + 1) + 1):
                j = f - e + 1
                term = mm(wm[e + 2], pro[e + 2, :, j * w : (j + 1) * w])
                total = term if total is None else total + term
            out[:, (f + 3) * w : (f + 4) * w] = total
            cb[t if short else f + 3] = total.astype(BF16)

        @pl.when(jnp.logical_not(inside))
        def _(f=f):
            out[:, (f + 3) * w : (f + 4) * w] = jnp.zeros((w, w), F32)
            if not short:
                cb[f + 3] = jnp.zeros((w, w), BF16)


def scatter_kernel(
    n, parts, groups, tile, cb, t2s, t2t, out, term, mine, rx1, tx2, rx2,
    send1, recv1, send2, recv2,
):
    s, p = lax.axis_index("slab"), lax.axis_index("piece")
    chips = groups // 2
    odd = lax.rem(p, 2)
    chip = p // 2
    sibling = p + 1 - 2 * odd
    gw = groups * tile
    mates = [2 * lax.rem(chip + o, chips) + odd for o in range(1, chips)]

    barrier = pltpu.get_barrier_semaphore()
    for mate in [sibling] + mates:
        pl.semaphore_signal(barrier, inc=1, device_id=(s, mate), device_id_type=MESH)
    if n < 7:
        out[...] = jnp.zeros_like(out)
    pl.semaphore_wait(barrier, chips)

    def pair_copy(m):
        return pltpu.make_async_remote_copy(
            src_ref=term.at[m, 1 - odd],
            dst_ref=rx1.at[m],
            send_sem=send1.at[m],
            recv_sem=recv1.at[m],
            device_id=(s, sibling),
            device_id_type=MESH,
        )

    def chip_copy(m, o):
        return pltpu.make_async_remote_copy(
            src_ref=tx2.at[m, o - 1],
            dst_ref=rx2.at[m, o - 1],
            send_sem=send2.at[m, o - 1],
            recv_sem=recv2.at[m, o - 1],
            device_id=(s, mates[o - 1]),
            device_id_type=MESH,
        )

    def pair_sum(m):
        pair_copy(m).wait_recv()
        for o in range(1, chips):
            h = lax.rem(chip + o, chips)
            tx2[m, o - 1] = (term[m, odd, h].astype(F32) + rx1[m, h].astype(F32)).astype(BF16)
            chip_copy(m, o).start()
        mine[m] = term[m, odd, chip].astype(F32) + rx1[m, chip].astype(F32)

    for m in range(parts):
        v = m if n < 7 else jnp.clip(s + m - 3, 0, n - 1)
        left = mm(t2t[...], cb[m]).astype(BF16)
        both = mm(left, t2s[v]).astype(BF16)
        for g in range(groups):
            term[m, g % 2, g // 2] = both[g * tile : (g + 1) * tile, :]
        pair_copy(m).start()
        if m > 0:
            pair_sum(m - 1)
    pair_sum(parts - 1)
    for m in range(parts):
        total = mine[m]
        for o in range(1, chips):
            chip_copy(m, o).wait_recv()
            total = total + rx2[m, o - 1].astype(F32)
        place = (m + 3 - s) * gw if n < 7 else m * gw
        out[:, pl.ds(pl.multiple_of(place, LANES), gw)] = total
    for m in range(parts):
        pair_copy(m).wait_send()
        for o in range(1, chips):
            chip_copy(m, o).wait_send()


def per_device(
    fine_tiles, fine_cols, bond_mask, diag_inv, tentative, aggregate, tentative_two, aggregate_two
):
    blocks, tile = diag_inv.shape[0], diag_inv.shape[1]
    slots = fine_cols.shape[1]
    aggs = tentative_two.shape[0]
    n, groups = lax.axis_size("slab"), lax.axis_size("piece")
    rows, w, gw = blocks * tile, aggs * tile, groups * tile
    parts = min(7, n)
    vmem = pl.BlockSpec(memory_space=pltpu.VMEM)
    smem = pl.BlockSpec(memory_space=pltpu.SMEM)
    shape = jax.ShapeDtypeStruct

    width = -(-blocks * slots // LANES) * LANES

    def line(x):
        x = x.reshape(1, -1)
        return jnp.pad(x, ((0, 0), (0, width - x.shape[1])))

    ints = jnp.concatenate([line(fine_cols), line(bond_mask), line(aggregate), line(aggregate_two)], 0)
    ints = jnp.pad(ints, ((0, 4), (0, 0)))

    far = min(3, n - 1)
    ag, dg, tg, ig = pl.pallas_call(
        functools.partial(gather_kernel, n, far),
        out_shape=(
            shape((n, rows, slots * tile), BF16),
            shape((n, rows // 2, 2 * tile), BF16),
            shape((n, rows, 2 * tile), BF16),
            shape((n, 8, width), jnp.int32),
        ),
        in_specs=[vmem] * 5,
        out_specs=(vmem,) * 4,
        scratch_shapes=[
            pltpu.SemaphoreType.DMA((2, far, 4)),
            pltpu.SemaphoreType.DMA((2, far, 4)),
        ],
        compiler_params=pltpu.CompilerParams(
            collective_id=0, has_side_effects=True, vmem_limit_bytes=VMEM_LIMIT
        ),
    )(
        fine_tiles.reshape(rows, slots * tile),
        diag_inv.reshape(rows, tile),
        tentative.reshape(rows, tile),
        tentative_two.reshape(w, tile),
        ints,
    )

    slab = lax.axis_index("slab").astype(jnp.int32).reshape(1)
    coarse, cb, t2s, t2t = pl.pallas_call(
        functools.partial(level_kernel, n, blocks, slots, aggs, groups, tile),
        out_shape=(
            shape((w, 7 * w), F32),
            shape((parts, w, w), BF16),
            shape((n, w, gw), BF16),
            shape((gw, w), BF16),
        ),
        in_specs=[smem, smem, vmem, vmem, vmem],
        out_specs=(vmem,) * 4,
        scratch_shapes=[
            pltpu.VMEM((5, rows, 3 * rows), BF16),
            pltpu.VMEM((rows, 3 * rows), BF16),
            pltpu.VMEM((5, rows, 3 * w), BF16),
            pltpu.VMEM((n, rows, w), BF16),
            pltpu.VMEM((tile, 3 * rows), F32),
            pltpu.VMEM((rows // 2, rows // 2), BF16),
            pltpu.VMEM((5, w, rows), BF16),
        ],
        compiler_params=pltpu.CompilerParams(vmem_limit_bytes=VMEM_LIMIT),
    )(slab, ig, ag, dg, tg)

    chips = groups // 2
    level_two = pl.pallas_call(
        functools.partial(scatter_kernel, n, parts, groups, tile),
        out_shape=shape((tile, 7 * gw), F32),
        in_specs=[vmem] * 3,
        out_specs=vmem,
        scratch_shapes=[
            pltpu.VMEM((parts, 2, chips, tile, gw), BF16),
            pltpu.VMEM((parts, tile, gw), F32),
            pltpu.VMEM((parts, chips, tile, gw), BF16),
            pltpu.VMEM((parts, chips - 1, tile, gw), BF16),
            pltpu.VMEM((parts, chips - 1, tile, gw), BF16),
            pltpu.SemaphoreType.DMA((parts,)),
            pltpu.SemaphoreType.DMA((parts,)),
            pltpu.SemaphoreType.DMA((parts, chips - 1)),
            pltpu.SemaphoreType.DMA((parts, chips - 1)),
        ],
        compiler_params=pltpu.CompilerParams(
            collective_id=1, has_side_effects=True, vmem_limit_bytes=VMEM_LIMIT
        ),
    )(cb, t2s, t2t)

    return (coarse.reshape(aggs, tile, 7 * w), level_two.reshape(1, tile, 7 * gw))


def solution(mesh):
    placed = (
        P(("slab", "piece"), None, None),
        P(("slab", "piece"), None),
        P(("slab", "piece"), None),
        P(("slab", "piece"), None, None),
        P(("slab", "piece"), None, None),
        P(("slab", "piece")),
        P(("slab", "piece"), None, None),
        P(("slab", "piece")),
    )
    return jax.shard_map(
        per_device,
        mesh=mesh,
        in_specs=placed,
        out_specs=(P(("slab", "piece"), None, None), P(("slab", "piece"), None, None)),
        check_vma=False,
    )
```

time: 433 us -> 91.8 us (0.21)
  waiting for transfers between devices: 186 us -> 0 us
  local copies, waits for them, and re-layouts: 127 us -> 4.3 us
  Pallas kernels: 0 us -> 85.9 us
  matrix products: 56.7 us -> 0 us
  other arithmetic: 27 us -> 0.68 us
  starting transfers between devices: 19.9 us -> 0 us
  between operations: 14.7 us -> 0.65 us
    ppermute x6 -> x0, waiting for transfers between devices: 110 us -> none  [the longest x2 47.4 us: padded_2(): lax.ppermute(tail, axis, [(i, (i + 1) % count) for i in range(ends)])]
    pallas_call x0 -> x3, Pallas kernels: none -> 85.9 us  [the longest x1 42.2 us: per_device(): pl.pallas_call(functools.partial(gather_kernel, n, far), out_shape=(shape...]
    psum x1 -> x0, waiting for transfers between devices: 75.5 us -> none  [per_device(): lax.psum(partial_value.astype(jnp.bfloat16), 'piece').astype(jnp.float32)]
    dot_general x21 -> x0, matrix products: 56.7 us -> none  [the longest x1 20.7 us: level_partial(): both = jnp.einsum('asobt,obtq->asoq', left, right, precision=EXACT_MODE)]
    gather x16 -> x0, local copies, waits for them, and re-layouts: 41.1 us -> none  [the longest x8 30.9 us: apply_rows(): rows_in = jnp.take(prolong_rim, column, axis=0)]
    scatter-add x1 -> x0, local copies, waits for them, and re-layouts: 21 us -> none  [prolong_rows(): summed = summed.at[:, :, 1, :].add(own_slot.astype(jnp.float32))]
    ppermute x6 -> x0, starting transfers between devices: 19.8 us -> none  [the longest x2 9.69 us: padded_2(): lax.ppermute(tail, axis, [(i, (i + 1) % count) for i in range(ends)])]
    convert_element_type x13 -> x0, local copies, waits for them, and re-layouts: 15.6 us -> none  [the longest x2 11.7 us: per_device(): partial_value.astype(jnp.bfloat16)]
  transfers between devices with their start and end apart: 8 -> 0, of which waited for: 7 -> 0; matrix products, arithmetic and copies ran while one was open for 21% -> 0% of each run, Pallas kernels for 0% -> 0%
where the time goes in v1:
time: 91.8 us; the launch traced here: 91.5 us
  Pallas kernels  85.9 us (94%)
  local copies, waits for them, and re-layouts  4.3 us (5%)
    pallas_call x1, Pallas kernels, per_device(): pl.pallas_call(functools.partial(gather_kernel, n, far), out_shape=(shape...  42.2 us
    pallas_call x1, Pallas kernels, per_device(): pl.pallas_call(functools.partial(level_kernel, n, blocks, slots, aggs, gr...  22.9 us
    pallas_call x1, Pallas kernels, per_device(): pl.pallas_call(functools.partial(scatter_kernel, n, parts, groups, tile),...  20.8 us
    unnamed x1, local copies, waits for them, and re-layouts  2.17 us

profile of v1, /device:TPU:0, one launch (start us, length us, event | category | flops | bytes accessed | tf_op | source)
XLA Modules:
  0.0 91.5 jit_solution(9621925898185222440)
XLA Ops:
  0.6 0.8 reshape.42
  1.4 0.8 reshape.43
  2.2 0.7 pad_add_fusion
  2.9 0.6 pad.22.i_ref
  3.5 42.2 %shard_map.95 = (bf16[4,512,512]{2,1,0:T(8,128)(2,1)}, bf16[4,256,128]{2,1,0:T(8,128)(2,1)}, bf16[4,512,128]{2,1,0:T(8,128)(2,1)}, s32[4,8,128]{2,1,0:T(8,128)}) custom-call(bf16[512,512]{1,0:T(8,128)(2,1)} %bitcast.10, bf16[512,64]{1,0:T(8,128)(2,1)} %bitcast.11, bf16[512,64]{1,0:T(8,128)(2,1)} %bitcast.12, bf16[512,64]{1,0:T(8,128)(2,1)} %bitcast.13, ...), custom_call_target="tpu_custom_call" | custom-call | tf_op jit(solution)/shard_map/pallas_call | solution.py:308
  45.7 22.9 %shard_map.96 = (f32[512,3584]{1,0:T(8,128)}, bf16[4,512,512]{2,1,0:T(8,128)(2,1)}, bf16[4,512,512]{2,1,0:T(8,128)(2,1)}, bf16[512,512]{1,0:T(8,128)(2,1)}) custom-call(s32[1]{0:T(128)} %bitcast.s_ref, s32[4,8,128]{2,1,0:T(8,128)} %get-tuple-element.10.i_ref, bf16[4,512,512]{2,1,0:T(8,128)(2,1)} %get-tuple-element.11.ag, ...), custom_call_target="tpu_custom_call" | custom-call | tf_op jit(solution)/shard_map/pallas_call | solution.py:334
  68.6 20.8 %shard_map.97 = f32[64,3584]{1,0:T(8,128)} custom-call(bf16[4,512,512]{2,1,0:T(8,128)(2,1)} %get-tuple-element.15.cb, bf16[4,512,512]{2,1,0:T(8,128)(2,1)} %get-tuple-element.16.t2s, bf16[512,512]{1,0:T(8,128)(2,1)} %get-tuple-element.17.t2t), custom_call_target="tpu_custom_call" | custom-call | tf_op jit(solution)/shard_map/pallas_call | solution.py:357
  89.3 2.2 %copy.11 = f32[1,64,3584]{2,1,0:T(8,128)} copy(f32[1,64,3584]{2,1,0:T(8,128)} %bitcast.9) | data formatting | bytes 1835008

commit v2 on v1

--- a/solution.py
+++ b/solution.py
@@ -2,6 +2,7 @@
 
 import jax
 import jax.numpy as jnp
+import numpy as np
 from jax import lax
 from jax.experimental import pallas as pl
 from jax.experimental.pallas import tpu as pltpu
@@ -10,7 +11,8 @@
 DAMPING = 2.0 / 3.0
 LANES = 128
 MESH = pl.DeviceIdType.MESH
-VMEM_LIMIT = 56 * 1024 * 1024
+VMEM_LIMIT = 60 * 1024 * 1024
+FUSED_LIMIT = 50 * 1024 * 1024
 F32 = jnp.float32
 BF16 = jnp.bfloat16
 
@@ -282,7 +284,7 @@
             chip_copy(m, o).wait_send()
 
 
-def per_device(
+def in_stages(
     fine_tiles, fine_cols, bond_mask, diag_inv, tentative, aggregate, tentative_two, aggregate_two
 ):
     blocks, tile = diag_inv.shape[0], diag_inv.shape[1]
@@ -378,6 +380,381 @@
     return (coarse.reshape(aggs, tile, 7 * w), level_two.reshape(1, tile, 7 * gw))
 
 
+def whole_kernel(
+    n, blocks, slots, aggs, groups, tile,
+    a_ref, d_ref, t_ref, q_ref, c_ref, out, two,
+    ag, dg, tg, cg, ad, sd, pro, ts, t2s, t2t, hot, bd, wm, cf, term, mine, rx1, tx2, rx2,
+    send_sem, recv_sem, out_sem, send1, recv1, send2, recv2,
+):
+    s, p = lax.axis_index("slab"), lax.axis_index("piece")
+    far = min(3, n - 1)
+    rows, w, gw = blocks * tile, aggs * tile, groups * tile
+    pair, half = 2 * tile, blocks // 2
+    chips = groups // 2
+    odd, chip = lax.rem(p, 2), p // 2
+    sibling = p + 1 - 2 * odd
+    mates = [2 * lax.rem(chip + o, chips) + odd for o in range(1, chips)]
+    barrier = pltpu.get_barrier_semaphore()
+
+    @pl.when(s > 0)
+    def _():
+        pl.semaphore_signal(barrier, inc=1, device_id=(s - 1, p), device_id_type=MESH)
+
+    @pl.when(s < n - 1)
+    def _():
+        pl.semaphore_signal(barrier, inc=1, device_id=(s + 1, p), device_id_type=MESH)
+
+    for mate in [sibling] + mates:
+        pl.semaphore_signal(barrier, inc=1, device_id=(s, mate), device_id_type=MESH)
+
+    cg[s] = c_ref[...]
+    tg[s] = jnp.concatenate([t_ref[...], q_ref[...]], axis=1)
+    dg[s] = jnp.concatenate([d_ref[0 : rows // 2, :], d_ref[rows // 2 : rows, :]], axis=1)
+    ag[s] = a_ref[...]
+    peers = chips + jnp.where(s > 0, 1, 0) + jnp.where(s < n - 1, 1, 0)
+    pl.semaphore_wait(barrier, peers)
+
+    arrays = (cg, tg, dg, ag)
+    reach = (far, far, min(2, far), min(2, far))
+
+    def valid(e):
+        return (s + e >= 0) & (s + e < n)
+
+    def copy(way, step, which, slab):
+        return pltpu.make_async_remote_copy(
+            src_ref=arrays[which].at[slab],
+            dst_ref=arrays[which].at[slab],
+            send_sem=send_sem.at[way, step, which],
+            recv_sem=recv_sem.at[way, step, which],
+            device_id=(s + 1 if way == 0 else s - 1, p),
+            device_id_type=MESH,
+        )
+
+    def send(way, step, which, act):
+        if step >= reach[which]:
+            return
+        slab = s - step if way == 0 else s + step
+        ok = valid(-step) & valid(1) if way == 0 else valid(step) & valid(-1)
+
+        @pl.when(ok)
+        def _():
+            act(copy(way, step, which, slab))
+
+    def start(c):
+        c.start()
+
+    def take(e, which):
+        if abs(e) > reach[which]:
+            return
+        way, step = (0 if e < 0 else 1), abs(e) - 1
+
+        @pl.when(valid(e))
+        def _():
+            copy(way, step, which, s + e).wait_recv()
+
+        send(way, step + 1, which, start)
+
+    for which in range(4):
+        for way in range(2):
+            send(way, 0, which, start)
+
+    lane = lax.broadcasted_iota(jnp.int32, (tile, pair), 1) // tile
+    lane_f = lane.astype(F32)
+
+    def basis(e):
+        @pl.when(valid(e))
+        def _():
+            u = s + e
+            ids = cg[u, blocks * slots :, :].astype(F32)
+            for b in range(blocks):
+                x = tg[u, b * tile : (b + 1) * tile, :].astype(F32)
+                turned = pltpu.roll(x, tile, 1)
+                two_t = jnp.where(lane == 0, turned, x)
+                one_t = jnp.where(lane == 0, x, turned)
+                g1 = ids[b : b + 1, :]
+                for q in range(w // pair):
+                    ts[u, b * tile : (b + 1) * tile, q * pair : (q + 1) * pair] = jnp.where(
+                        lane_f + 2.0 * q == g1, one_t, 0.0
+                    ).astype(BF16)
+                g2 = ids[blocks + b : blocks + b + 1, :]
+                for q in range(gw // pair):
+                    t2s[u, b * tile : (b + 1) * tile, q * pair : (q + 1) * pair] = jnp.where(
+                        lane_f + 2.0 * q == g2, two_t, 0.0
+                    ).astype(BF16)
+
+    def build(e):
+        @pl.when(valid(e))
+        def _():
+            u = s + e
+            codes = cg[u, 0 : blocks * slots, :].astype(F32)
+            at = lax.broadcasted_iota(jnp.int32, (blocks * slots, pair), 1) // tile
+            at = at.astype(F32)
+            for cp in range(3 * rows // pair):
+                hit = jnp.where(codes == at + 2.0 * cp, 1.0, 0.0)
+                hot[:, :, cp * pair : (cp + 1) * pair] = hit.reshape(blocks, slots, pair)
+
+            def row(i, carry):
+                base = pl.multiple_of(i * tile, tile)
+                tiles = []
+                for k2 in range(slots // 2):
+                    x = ag[u, pl.ds(base, tile), k2 * pair : (k2 + 1) * pair].astype(F32)
+                    turned = pltpu.roll(x, tile, 1)
+                    for y in (jnp.where(lane == 0, x, turned), jnp.where(lane == 0, turned, x)):
+                        tiles.append(y.astype(BF16).reshape(tile // 16, 16, pair))
+                for cp in range(3 * rows // pair):
+                    total = None
+                    for k in range(slots):
+                        m = hot[i, k : k + 1, cp * pair : (cp + 1) * pair]
+                        m = jnp.broadcast_to(m, (16, pair)).astype(BF16)
+                        y = tiles[k] * m[None]
+                        total = y if total is None else total + y
+                    ad[e + 2, pl.ds(base, tile), cp * pair : (cp + 1) * pair] = total.reshape(tile, pair)
+                return carry
+
+            lax.fori_loop(0, blocks, row, 0)
+            for h in range(2):
+                for b in range(half):
+                    x = dg[u, b * tile : (b + 1) * tile, :].astype(F32)
+                    if b % 2 != h:
+                        x = pltpu.roll(x, tile, 1)
+                    bd[b * tile : (b + 1) * tile, (b // 2) * pair : (b // 2 + 1) * pair] = (
+                        jnp.where(lane == b % 2, x, 0.0).astype(BF16)
+                    )
+                lo = h * half * tile
+                hi = lo + half * tile
+                sd[lo:hi, :] = (DAMPING * mm(bd[...], ad[e + 2, lo:hi, :])).astype(BF16)
+
+        @pl.when(jnp.logical_not(valid(e)))
+        def _():
+            ad[e + 2] = jnp.zeros((rows, 3 * rows), BF16)
+
+    def prolong(e):
+        for j in range(3):
+            ok = valid(e) & valid(e + j - 1)
+
+            @pl.when(ok)
+            def _(j=j):
+                v = s + e + j - 1
+                value = -mm(sd[:, j * rows : (j + 1) * rows], ts[v])
+                if j == 1:
+                    value = value + ts[v].astype(F32)
+                pro[e + 2, :, j * w : (j + 1) * w] = value.astype(BF16)
+
+            @pl.when(jnp.logical_not(ok))
+            def _(j=j):
+                pro[e + 2, :, j * w : (j + 1) * w] = jnp.zeros((rows, w), BF16)
+
+    def pair_copy(m):
+        return pltpu.make_async_remote_copy(
+            src_ref=term.at[m, 1 - odd],
+            dst_ref=rx1.at[m],
+            send_sem=send1.at[m],
+            recv_sem=recv1.at[m],
+            device_id=(s, sibling),
+            device_id_type=MESH,
+        )
+
+    def chip_copy(m, o):
+        return pltpu.make_async_remote_copy(
+            src_ref=tx2.at[m, o - 1],
+            dst_ref=rx2.at[m, o - 1],
+            send_sem=send2.at[m, o - 1],
+            recv_sem=recv2.at[m, o - 1],
+            device_id=(s, mates[o - 1]),
+            device_id_type=MESH,
+        )
+
+    def leave(f):
+        return pltpu.make_async_copy(
+            cf.at[f + 3], out.at[:, pl.ds((f + 3) * w, w)], out_sem.at[f + 3]
+        )
+
+    def coarse(f):
+        m = f + 3
+
+        @pl.when(valid(f))
+        def _():
+            total = None
+            for e in range(max(-2, f - 1), min(2, f + 1) + 1):
+                j = f - e + 1
+                part = mm(wm[e + 2], pro[e + 2, :, j * w : (j + 1) * w])
+                total = part if total is None else total + part
+            cf[m] = total
+            leave(f).start()
+            left = mm(t2t[...], total.astype(BF16)).astype(BF16)
+            both = mm(left, t2s[s + f]).astype(BF16)
+            for g in range(groups):
+                term[m, g % 2, g // 2] = both[g * tile : (g + 1) * tile, :]
+            pair_copy(m).start()
+
+    def pair_sum(f):
+        m = f + 3
+
+        @pl.when(valid(f))
+        def _():
+            pair_copy(m).wait_recv()
+            for o in range(1, chips):
+                h = lax.rem(chip + o, chips)
+                tx2[m, o - 1] = (term[m, odd, h].astype(F32) + rx1[m, h].astype(F32)).astype(BF16)
+                chip_copy(m, o).start()
+            mine[m] = term[m, odd, chip].astype(F32) + rx1[m, chip].astype(F32)
+
+    bd[...] = jnp.zeros_like(bd)
+    for f in range(-3, 4):
+
+        @pl.when(jnp.logical_not(valid(f)))
+        def _(f=f):
+            cf[f + 3] = jnp.zeros((w, w), F32)
+            leave(f).start()
+            two[:, (f + 3) * gw : (f + 4) * gw] = jnp.zeros((tile, gw), F32)
+
+    basis(0)
+    t2t[...] = t2s[s].astype(F32).T.astype(BF16)
+    build(0)
+    for e in (-1, 1):
+        take(e, 0)
+        take(e, 1)
+        basis(e)
+    prolong(0)
+    for e in (-1, 1):
+        take(e, 2)
+        take(e, 3)
+    for e in (-2, 2):
+        take(e, 0)
+        take(e, 1)
+        basis(e)
+    for e in (-1, 1):
+        build(e)
+        prolong(e)
+    turned = [
+        pro[dj + 2, :, (1 - dj) * w : (2 - dj) * w].astype(F32).T.astype(BF16) for dj in (-1, 0, 1)
+    ]
+    for e in range(-2, 3):
+        total = None
+        for dj in (-1, 0, 1):
+            j = e - dj + 1
+            if 0 <= j < 3:
+                part = mm(turned[dj + 1], ad[dj + 2, :, j * rows : (j + 1) * rows])
+                total = part if total is None else total + part
+        wm[e + 2] = total.astype(BF16)
+    coarse(0)
+    for e in (-3, 3):
+        take(e, 0)
+        take(e, 1)
+        basis(e)
+    order = [0]
+    for way in (-1, 1):
+        take(2 * way, 2)
+        take(2 * way, 3)
+        build(2 * way)
+        prolong(2 * way)
+        for f in (way, 2 * way, 3 * way):
+            coarse(f)
+            pair_sum(order[-1])
+            order.append(f)
+    pair_sum(order[-1])
+    for f in order:
+        m = f + 3
+
+        @pl.when(valid(f))
+        def _(m=m):
+            total = mine[m]
+            for o in range(1, chips):
+                chip_copy(m, o).wait_recv()
+                total = total + rx2[m, o - 1].astype(F32)
+            two[:, m * gw : (m + 1) * gw] = total
+
+    for f in range(-3, 4):
+        m = f + 3
+        leave(f).wait()
+
+        @pl.when(valid(f))
+        def _(m=m):
+            pair_copy(m).wait_send()
+            for o in range(1, chips):
+                chip_copy(m, o).wait_send()
+
+    for step in range(far):
+        for which in range(4):
+            for way in range(2):
+                send(way, step, which, lambda c: c.wait_send())
+
+
+def at_once(
+    fine_tiles, fine_cols, bond_mask, diag_inv, tentative, aggregate, tentative_two, aggregate_two
+):
+    blocks, tile = diag_inv.shape[0], diag_inv.shape[1]
+    slots = fine_cols.shape[1]
+    aggs = tentative_two.shape[0]
+    n, groups = lax.axis_size("slab"), lax.axis_size("piece")
+    rows, w, gw = blocks * tile, aggs * tile, groups * tile
+    pair, chips, far = 2 * tile, groups // 2, min(3, n - 1)
+    codes = jnp.concatenate(
+        [jnp.where(bond_mask != 0, fine_cols, -1).reshape(-1), aggregate, aggregate_two]
+    )
+    codes = jnp.broadcast_to(codes.astype(BF16)[:, None], (codes.shape[0], pair))
+    vmem = pl.BlockSpec(memory_space=pltpu.VMEM)
+    dma = pltpu.SemaphoreType.DMA
+    scratch = [
+        pltpu.VMEM((n, rows, slots * tile), BF16),
+        pltpu.VMEM((n, rows // 2, pair), BF16),
+        pltpu.VMEM((n, rows, pair), BF16),
+        pltpu.VMEM((n, codes.shape[0], pair), BF16),
+        pltpu.VMEM((5, rows, 3 * rows), BF16),
+        pltpu.VMEM((rows, 3 * rows), BF16),
+        pltpu.VMEM((5, rows, 3 * w), BF16),
+        pltpu.VMEM((n, rows, w), BF16),
+        pltpu.VMEM((n, w, gw), BF16),
+        pltpu.VMEM((gw, w), BF16),
+        pltpu.VMEM((blocks, slots, 3 * rows), F32),
+        pltpu.VMEM((rows // 2, rows // 2), BF16),
+        pltpu.VMEM((5, w, rows), BF16),
+        pltpu.VMEM((7, w, w), F32),
+        pltpu.VMEM((7, 2, chips, tile, gw), BF16),
+        pltpu.VMEM((7, tile, gw), F32),
+        pltpu.VMEM((7, chips, tile, gw), BF16),
+        pltpu.VMEM((7, chips - 1, tile, gw), BF16),
+        pltpu.VMEM((7, chips - 1, tile, gw), BF16),
+    ]
+    size = sum(x.dtype.itemsize * np.prod(x.shape) for x in scratch)
+    if size > FUSED_LIMIT:
+        return None
+    coarse, level_two = pl.pallas_call(
+        functools.partial(whole_kernel, n, blocks, slots, aggs, groups, tile),
+        out_shape=(
+            jax.ShapeDtypeStruct((w, 7 * w), F32),
+            jax.ShapeDtypeStruct((tile, 7 * gw), F32),
+        ),
+        in_specs=[vmem] * 5,
+        out_specs=(pl.BlockSpec(memory_space=pl.ANY), vmem),
+        scratch_shapes=scratch
+        + [
+            dma((2, far, 4)),
+            dma((2, far, 4)),
+            dma((7,)),
+            dma((7,)),
+            dma((7,)),
+            dma((7, chips - 1)),
+            dma((7, chips - 1)),
+        ],
+        compiler_params=pltpu.CompilerParams(
+            collective_id=2, has_side_effects=True, vmem_limit_bytes=VMEM_LIMIT
+        ),
+    )(
+        fine_tiles.reshape(rows, slots * tile),
+        diag_inv.reshape(rows, tile),
+        tentative.reshape(rows, tile),
+        tentative_two.reshape(w, tile),
+        codes,
+    )
+    return (coarse.reshape(aggs, tile, 7 * w), level_two.reshape(1, tile, 7 * gw))
+
+
+def per_device(*args):
+    done = at_once(*args)
+    return in_stages(*args) if done is None else done
+
+
 def solution(mesh):
     placed = (
         P(("slab", "piece"), None, None),

time: 91.8 us -> 73 us (0.80)
  Pallas kernels: 85.9 us -> 61.6 us
  local copies, waits for them, and re-layouts: 4.3 us -> 8.39 us
  other arithmetic: 0.68 us -> 2.1 us
    pallas_call x3 -> x1, Pallas kernels: 85.9 us -> 61.6 us  [at_once(): pl.pallas_call(functools.partial(whole_kernel, n, blocks, slots, aggs, gr...]
    unnamed x1 -> x4, local copies, waits for them, and re-layouts: 2.17 us -> 7.61 us
    another operation x0 -> x3, other arithmetic: none -> 2.02 us
    reshape x2 -> x0, local copies, waits for them, and re-layouts: 1.53 us -> none  [line(): x = x.reshape(1, -1)]
where the time goes in v2:
time: 73 us; the launch traced here: 72.7 us
  Pallas kernels  61.6 us (84%)
  local copies, waits for them, and re-layouts  8.39 us (11%)
  other arithmetic  2.1 us (3%)
    pallas_call x1, Pallas kernels, at_once(): pl.pallas_call(functools.partial(whole_kernel, n, blocks, slots, aggs, gr...  61.6 us
    unnamed x4, local copies, waits for them, and re-layouts  7.61 us
    another operation x3, other arithmetic  2.02 us

profile of v2, /device:TPU:0, one launch (start us, length us, event | category | flops | bytes accessed | tf_op | source)
XLA Modules:
  0.0 72.7 jit_solution(11009803685011537845)
XLA Ops:
  0.6 0.7 convert.11
  1.3 0.7 convert.12
  1.9 0.7 select_convert_fusion
  2.7 0.1 concatenate.10
  2.7 0.1 pad_maximum_fusion
  2.8 0.7 broadcast_in_dim.11.c_ref
  3.5 61.6 %shard_map.95 = (f32[512,3584]{1,0:T(8,128)}, f32[64,3584]{1,0:T(8,128)}) custom-call(bf16[512,512]{1,0:T(8,128)(2,1)} %bitcast.8, bf16[512,64]{1,0:T(8,128)(2,1)} %bitcast.9, bf16[512,64]{1,0:T(8,128)(2,1)} %bitcast.10, bf16[512,64]{1,0:T(8,128)(2,1)} %bitcast.11, bf16[80,128]{1,0:T(8,128)(2,1)} %broadcast_in_dim.11.c_ref), custom_call_target="tpu_custom_call" | custom-call | tf_op jit(solution)/shard_map/pallas_call | solution.py:722
  65.1 0.0 copy-start
  65.1 6.7 %copy.12 = f32[8,64,3584]{2,1,0:T(8,128)} copy(f32[8,64,3584]{2,1,0:T(8,128)} %bitcast.6) | data formatting | bytes 14680064
  71.8 0.0 copy-done
  71.8 0.9 %copy.13 = f32[1,64,3584]{2,1,0:T(8,128)} copy(f32[1,64,3584]{2,1,0:T(8,128)S(1)} %bitcast.7) | data formatting | bytes 1835008
Async XLA Ops:
  65.1 6.7 %copy-start = (f32[64,3584]{1,0:T(8,128)S(1)}, f32[64,3584]{1,0:T(8,128)}, u32[]{:S(2)}) copy-start(f32[64,3584]{1,0:T(8,128)} %get-tuple-element.5) | copy-start | bytes 2752516

commit v3 on v2

--- a/solution.py
+++ b/solution.py
@@ -382,8 +382,8 @@
 
 def whole_kernel(
     n, blocks, slots, aggs, groups, tile,
-    a_ref, d_ref, t_ref, q_ref, c_ref, out, two,
-    ag, dg, tg, cg, ad, sd, pro, ts, t2s, t2t, hot, bd, wm, cf, term, mine, rx1, tx2, rx2,
+    a_ref, d_ref, t_ref, q_ref, cols_ref, mask_ref, one_ref, two_ref, out, two,
+    ag, dg, tg, cg, ad, sd, pro, ts, t2s, t2t, hot, ids, bd, wm, cf, term, mine, rx1, tx2, rx2,
     send_sem, recv_sem, out_sem, send1, recv1, send2, recv2,
 ):
     s, p = lax.axis_index("slab"), lax.axis_index("piece")
@@ -407,23 +407,35 @@
     for mate in [sibling] + mates:
         pl.semaphore_signal(barrier, inc=1, device_id=(s, mate), device_id_type=MESH)
 
-    cg[s] = c_ref[...]
+    for i in range(blocks):
+        for k in range(slots):
+            code = jnp.where(mask_ref[i, k] != 0, cols_ref[i, k], -1)
+            ids[i * slots + k : i * slots + k + 1, :] = jnp.full((1, pair), code, jnp.int32)
+        at = blocks * slots + i
+        ids[at : at + 1, :] = jnp.full((1, pair), one_ref[i], jnp.int32)
+        ids[at + blocks : at + blocks + 1, :] = jnp.full((1, pair), two_ref[i], jnp.int32)
+    cg[s] = ids[...].astype(F32).astype(BF16)
     tg[s] = jnp.concatenate([t_ref[...], q_ref[...]], axis=1)
     dg[s] = jnp.concatenate([d_ref[0 : rows // 2, :], d_ref[rows // 2 : rows, :]], axis=1)
     ag[s] = a_ref[...]
     peers = chips + jnp.where(s > 0, 1, 0) + jnp.where(s < n - 1, 1, 0)
     pl.semaphore_wait(barrier, peers)
 
-    arrays = (cg, tg, dg, ag)
-    reach = (far, far, min(2, far), min(2, far))
+    kinds = 5
+    reach = (far, far) + (min(2, far),) * 3
+
+    def part_of(which, slab):
+        if which < 3:
+            return (cg, tg, dg)[which].at[slab]
+        return ag.at[slab, pl.ds((which - 3) * (rows // 2), rows // 2)]
 
     def valid(e):
         return (s + e >= 0) & (s + e < n)
 
     def copy(way, step, which, slab):
         return pltpu.make_async_remote_copy(
-            src_ref=arrays[which].at[slab],
-            dst_ref=arrays[which].at[slab],
+            src_ref=part_of(which, slab),
+            dst_ref=part_of(which, slab),
             send_sem=send_sem.at[way, step, which],
             recv_sem=recv_sem.at[way, step, which],
             device_id=(s + 1 if way == 0 else s - 1, p),
@@ -454,7 +466,7 @@
 
         send(way, step + 1, which, start)
 
-    for which in range(4):
+    for which in range(kinds):
         for way in range(2):
             send(way, 0, which, start)
 
@@ -465,33 +477,36 @@
         @pl.when(valid(e))
         def _():
             u = s + e
-            ids = cg[u, blocks * slots :, :].astype(F32)
+            names = cg[u, blocks * slots :, :].astype(F32)
             for b in range(blocks):
                 x = tg[u, b * tile : (b + 1) * tile, :].astype(F32)
                 turned = pltpu.roll(x, tile, 1)
                 two_t = jnp.where(lane == 0, turned, x)
                 one_t = jnp.where(lane == 0, x, turned)
-                g1 = ids[b : b + 1, :]
+                g1 = names[b : b + 1, :]
                 for q in range(w // pair):
                     ts[u, b * tile : (b + 1) * tile, q * pair : (q + 1) * pair] = jnp.where(
                         lane_f + 2.0 * q == g1, one_t, 0.0
                     ).astype(BF16)
-                g2 = ids[blocks + b : blocks + b + 1, :]
+                g2 = names[blocks + b : blocks + b + 1, :]
                 for q in range(gw // pair):
                     t2s[u, b * tile : (b + 1) * tile, q * pair : (q + 1) * pair] = jnp.where(
                         lane_f + 2.0 * q == g2, two_t, 0.0
                     ).astype(BF16)
 
-    def build(e):
+    def build(e, h):
+        lo, hi = h * half * tile, (h + 1) * half * tile
+
         @pl.when(valid(e))
         def _():
             u = s + e
-            codes = cg[u, 0 : blocks * slots, :].astype(F32)
-            at = lax.broadcasted_iota(jnp.int32, (blocks * slots, pair), 1) // tile
-            at = at.astype(F32)
-            for cp in range(3 * rows // pair):
-                hit = jnp.where(codes == at + 2.0 * cp, 1.0, 0.0)
-                hot[:, :, cp * pair : (cp + 1) * pair] = hit.reshape(blocks, slots, pair)
+            if h == 0:
+                codes = cg[u, 0 : blocks * slots, :].astype(F32)
+                at = lax.broadcasted_iota(jnp.int32, (blocks * slots, pair), 1) // tile
+                at = at.astype(F32)
+                for cp in range(3 * rows // pair):
+                    hit = jnp.where(codes == at + 2.0 * cp, 1.0, 0.0)
+                    hot[:, :, cp * pair : (cp + 1) * pair] = hit.reshape(blocks, slots, pair)
 
             def row(i, carry):
                 base = pl.multiple_of(i * tile, tile)
@@ -511,38 +526,36 @@
                     ad[e + 2, pl.ds(base, tile), cp * pair : (cp + 1) * pair] = total.reshape(tile, pair)
                 return carry
 
-            lax.fori_loop(0, blocks, row, 0)
-            for h in range(2):
-                for b in range(half):
-                    x = dg[u, b * tile : (b + 1) * tile, :].astype(F32)
-                    if b % 2 != h:
-                        x = pltpu.roll(x, tile, 1)
-                    bd[b * tile : (b + 1) * tile, (b // 2) * pair : (b // 2 + 1) * pair] = (
-                        jnp.where(lane == b % 2, x, 0.0).astype(BF16)
-                    )
-                lo = h * half * tile
-                hi = lo + half * tile
-                sd[lo:hi, :] = (DAMPING * mm(bd[...], ad[e + 2, lo:hi, :])).astype(BF16)
-
-        @pl.when(jnp.logical_not(valid(e)))
-        def _():
-            ad[e + 2] = jnp.zeros((rows, 3 * rows), BF16)
-
-    def prolong(e):
-        for j in range(3):
-            ok = valid(e) & valid(e + j - 1)
-
-            @pl.when(ok)
-            def _(j=j):
-                v = s + e + j - 1
-                value = -mm(sd[:, j * rows : (j + 1) * rows], ts[v])
-                if j == 1:
-                    value = value + ts[v].astype(F32)
-                pro[e + 2, :, j * w : (j + 1) * w] = value.astype(BF16)
-
-            @pl.when(jnp.logical_not(ok))
-            def _(j=j):
-                pro[e + 2, :, j * w : (j + 1) * w] = jnp.zeros((rows, w), BF16)
+            lax.fori_loop(h * half, (h + 1) * half, row, 0)
+            for b in range(half):
+                x = dg[u, b * tile : (b + 1) * tile, :].astype(F32)
+                if b % 2 != h:
+                    x = pltpu.roll(x, tile, 1)
+                bd[b * tile : (b + 1) * tile, (b // 2) * pair : (b // 2 + 1) * pair] = (
+                    jnp.where(lane == b % 2, x, 0.0).astype(BF16)
+                )
+            sd[lo:hi, :] = (DAMPING * mm(bd[...], ad[e + 2, lo:hi, :])).astype(BF16)
+
+        if abs(e) < 2:
+
+            @pl.when(jnp.logical_not(valid(e)))
+            def _():
+                ad[e + 2, lo:hi, :] = jnp.zeros((hi - lo, 3 * rows), BF16)
+
+    def prolong(e, j, lo, hi):
+        ok = valid(e) & valid(e + j - 1)
+
+        @pl.when(ok)
+        def _():
+            v = s + e + j - 1
+            value = -mm(sd[lo:hi, j * rows : (j + 1) * rows], ts[v])
+            if j == 1:
+                value = value + ts[v, lo:hi, :].astype(F32)
+            pro[e + 2, lo:hi, j * w : (j + 1) * w] = value.astype(BF16)
+
+        @pl.when(jnp.logical_not(ok))
+        def _():
+            pro[e + 2, lo:hi, j * w : (j + 1) * w] = jnp.zeros((hi - lo, w), BF16)
 
     def pair_copy(m):
         return pltpu.make_async_remote_copy(
@@ -566,22 +579,35 @@
 
     def leave(f):
         return pltpu.make_async_copy(
-            cf.at[f + 3], out.at[:, pl.ds((f + 3) * w, w)], out_sem.at[f + 3]
+            cf.at[f + 3], out.at[f + 3], out_sem.at[f + 3]
         )
+
+    def sum_over(f, sides):
+        total = None
+        for e in sides:
+            j = f - e + 1
+            part = mm(wm[e + 2], pro[e + 2, :, j * w : (j + 1) * w])
+            total = part if total is None else total + part
+        return total
+
+    def early(f):
+        sides = [e for e in (-1, 0, 1) if abs(f - e) < 2]
+
+        @pl.when(valid(f))
+        def _():
+            cf[f + 3] = sum_over(f, sides)
 
     def coarse(f):
         m = f + 3
 
         @pl.when(valid(f))
         def _():
-            total = None
-            for e in range(max(-2, f - 1), min(2, f + 1) + 1):
-                j = f - e + 1
-                part = mm(wm[e + 2], pro[e + 2, :, j * w : (j + 1) * w])
-                total = part if total is None else total + part
-            cf[m] = total
+            if abs(f) == 3:
+                cf[m] = sum_over(f, [2 if f > 0 else -2])
+            elif f != 0:
+                cf[m] += sum_over(f, [2 if f > 0 else -2])
             leave(f).start()
-            left = mm(t2t[...], total.astype(BF16)).astype(BF16)
+            left = mm(t2t[...], cf[m].astype(BF16)).astype(BF16)
             both = mm(left, t2s[s + f]).astype(BF16)
             for g in range(groups):
                 term[m, g % 2, g // 2] = both[g * tile : (g + 1) * tile, :]
@@ -604,28 +630,32 @@
 
         @pl.when(jnp.logical_not(valid(f)))
         def _(f=f):
-            cf[f + 3] = jnp.zeros((w, w), F32)
-            leave(f).start()
             two[:, (f + 3) * gw : (f + 4) * gw] = jnp.zeros((tile, gw), F32)
 
     basis(0)
     t2t[...] = t2s[s].astype(F32).T.astype(BF16)
-    build(0)
+    build(0, 0)
+    build(0, 1)
     for e in (-1, 1):
         take(e, 0)
         take(e, 1)
         basis(e)
-    prolong(0)
-    for e in (-1, 1):
-        take(e, 2)
-        take(e, 3)
+    for j in range(3):
+        prolong(0, j, 0, rows)
+    for h in range(2):
+        for e in (-1, 1):
+            if h == 0:
+                take(e, 2)
+            take(e, 3 + h)
     for e in (-2, 2):
         take(e, 0)
         take(e, 1)
         basis(e)
     for e in (-1, 1):
-        build(e)
-        prolong(e)
+        build(e, 0)
+        build(e, 1)
+        for j in range(3):
+            prolong(e, j, 0, rows)
     turned = [
         pro[dj + 2, :, (1 - dj) * w : (2 - dj) * w].astype(F32).T.astype(BF16) for dj in (-1, 0, 1)
     ]
@@ -637,20 +667,30 @@
                 part = mm(turned[dj + 1], ad[dj + 2, :, j * rows : (j + 1) * rows])
                 total = part if total is None else total + part
         wm[e + 2] = total.astype(BF16)
+    early(0)
     coarse(0)
+    for f in (-2, -1, 1, 2):
+        early(f)
+    pair_sum(0)
     for e in (-3, 3):
         take(e, 0)
         take(e, 1)
         basis(e)
     order = [0]
     for way in (-1, 1):
-        take(2 * way, 2)
-        take(2 * way, 3)
-        build(2 * way)
-        prolong(2 * way)
+        e = 2 * way
+        take(e, 2)
+        take(e, 3)
+        build(e, 0)
+        for j in range(3):
+            prolong(e, j, 0, rows // 2)
+        take(e, 4)
+        build(e, 1)
         for f in (way, 2 * way, 3 * way):
+            prolong(e, f - e + 1, rows // 2, rows)
             coarse(f)
-            pair_sum(order[-1])
+            if order[-1] != 0:
+                pair_sum(order[-1])
             order.append(f)
     pair_sum(order[-1])
     for f in order:
@@ -666,18 +706,58 @@
 
     for f in range(-3, 4):
         m = f + 3
-        leave(f).wait()
 
         @pl.when(valid(f))
-        def _(m=m):
+        def _(f=f, m=m):
+            leave(f).wait()
             pair_copy(m).wait_send()
             for o in range(1, chips):
                 chip_copy(m, o).wait_send()
 
     for step in range(far):
-        for which in range(4):
+        for which in range(kinds):
             for way in range(2):
                 send(way, step, which, lambda c: c.wait_send())
+
+
+def place_kernel(n, blocks, level, out, two, held, zero, in_sem, out_sem):
+    s = lax.axis_index("slab")
+    w = zero.shape[0]
+
+    def write(f, source):
+        return pltpu.make_async_copy(source, out.at[:, pl.ds((f + 3) * w, w)], out_sem.at[f + 3])
+
+    def read(f):
+        return pltpu.make_async_copy(blocks.at[f + 3], held.at[f + 3], in_sem.at[f + 3])
+
+    def either(f, inside, outside):
+        ok = (s + f >= 0) & (s + f < n)
+
+        @pl.when(ok)
+        def _():
+            inside()
+
+        if outside is not None:
+
+            @pl.when(jnp.logical_not(ok))
+            def _():
+                outside()
+
+    for f in range(-3, 4):
+        either(f, lambda: read(f).start(), None)
+    zero[...] = jnp.zeros_like(zero)
+    for f in range(-3, 4):
+        either(f, lambda: None, lambda: write(f, zero).start())
+
+    def onward(f):
+        read(f).wait()
+        write(f, held.at[f + 3]).start()
+
+    for f in range(-3, 4):
+        either(f, lambda: onward(f), None)
+    two[...] = level[...]
+    for f in range(-3, 4):
+        either(f, lambda: write(f, held.at[f + 3]).wait(), lambda: write(f, zero).wait())
 
 
 def at_once(
@@ -689,17 +769,15 @@
     n, groups = lax.axis_size("slab"), lax.axis_size("piece")
     rows, w, gw = blocks * tile, aggs * tile, groups * tile
     pair, chips, far = 2 * tile, groups // 2, min(3, n - 1)
-    codes = jnp.concatenate(
-        [jnp.where(bond_mask != 0, fine_cols, -1).reshape(-1), aggregate, aggregate_two]
-    )
-    codes = jnp.broadcast_to(codes.astype(BF16)[:, None], (codes.shape[0], pair))
+    names = blocks * slots + 2 * blocks
     vmem = pl.BlockSpec(memory_space=pltpu.VMEM)
+    smem = pl.BlockSpec(memory_space=pltpu.SMEM)
     dma = pltpu.SemaphoreType.DMA
     scratch = [
         pltpu.VMEM((n, rows, slots * tile), BF16),
         pltpu.VMEM((n, rows // 2, pair), BF16),
         pltpu.VMEM((n, rows, pair), BF16),
-        pltpu.VMEM((n, codes.shape[0], pair), BF16),
+        pltpu.VMEM((n, names, pair), BF16),
         pltpu.VMEM((5, rows, 3 * rows), BF16),
         pltpu.VMEM((rows, 3 * rows), BF16),
         pltpu.VMEM((5, rows, 3 * w), BF16),
@@ -707,6 +785,7 @@
         pltpu.VMEM((n, w, gw), BF16),
         pltpu.VMEM((gw, w), BF16),
         pltpu.VMEM((blocks, slots, 3 * rows), F32),
+        pltpu.VMEM((names, pair), jnp.int32),
         pltpu.VMEM((rows // 2, rows // 2), BF16),
         pltpu.VMEM((5, w, rows), BF16),
         pltpu.VMEM((7, w, w), F32),
@@ -719,18 +798,18 @@
     size = sum(x.dtype.itemsize * np.prod(x.shape) for x in scratch)
     if size > FUSED_LIMIT:
         return None
-    coarse, level_two = pl.pallas_call(
+    held, level_two = pl.pallas_call(
         functools.partial(whole_kernel, n, blocks, slots, aggs, groups, tile),
         out_shape=(
-            jax.ShapeDtypeStruct((w, 7 * w), F32),
+            jax.ShapeDtypeStruct((7, w, w), F32),
             jax.ShapeDtypeStruct((tile, 7 * gw), F32),
         ),
-        in_specs=[vmem] * 5,
+        in_specs=[vmem] * 4 + [smem] * 4,
         out_specs=(pl.BlockSpec(memory_space=pl.ANY), vmem),
         scratch_shapes=scratch
         + [
-            dma((2, far, 4)),
-            dma((2, far, 4)),
+            dma((2, far, 5)),
+            dma((2, far, 5)),
             dma((7,)),
             dma((7,)),
             dma((7,)),
@@ -745,8 +824,27 @@
         diag_inv.reshape(rows, tile),
         tentative.reshape(rows, tile),
         tentative_two.reshape(w, tile),
-        codes,
+        fine_cols,
+        bond_mask,
+        aggregate,
+        aggregate_two,
     )
+    coarse, level_two = pl.pallas_call(
+        functools.partial(place_kernel, n),
+        out_shape=(
+            jax.ShapeDtypeStruct((w, 7 * w), F32),
+            jax.ShapeDtypeStruct((tile, 7 * gw), F32),
+        ),
+        in_specs=[pl.BlockSpec(memory_space=pl.ANY), vmem],
+        out_specs=(pl.BlockSpec(memory_space=pl.ANY), vmem),
+        scratch_shapes=[
+            pltpu.VMEM((7, w, w), F32),
+            pltpu.VMEM((w, w), F32),
+            dma((7,)),
+            dma((7,)),
+        ],
+        compiler_params=pltpu.CompilerParams(vmem_limit_bytes=VMEM_LIMIT),
+    )(held, level_two)
     return (coarse.reshape(aggs, tile, 7 * w), level_two.reshape(1, tile, 7 * gw))
 
 

time: 73 us -> 69.2 us (0.948)
  local copies, waits for them, and re-layouts: 8.39 us -> 0 us
  Pallas kernels: 61.6 us -> 68.2 us
  other arithmetic: 2.1 us -> 0 us
    unnamed x4 -> x0, local copies, waits for them, and re-layouts: 7.61 us -> none
    pallas_call x0 -> x1, Pallas kernels: none -> 7.1 us  [at_once(): pl.pallas_call(functools.partial(place_kernel, n), out_shape=(jax.ShapeDt...]
    another operation x3 -> x0, other arithmetic: 2.02 us -> none
where the time goes in v3:
time: 69.2 us; the launch traced here: 69 us
  Pallas kernels  68.2 us (99%)
  between operations  0.8 us (1%)
    pallas_call x1, Pallas kernels, at_once(): pl.pallas_call(functools.partial(whole_kernel, n, blocks, slots, aggs, gr...  61.1 us
    pallas_call x1, Pallas kernels, at_once(): pl.pallas_call(functools.partial(place_kernel, n), out_shape=(jax.ShapeDt...  7.1 us

profile of v3, /device:TPU:0, one launch (start us, length us, event | category | flops | bytes accessed | tf_op | source)
XLA Modules:
  0.0 69.0 jit_solution(16747762054001649907)
XLA Ops:
  0.6 61.1 %shard_map.95 = (f32[7,512,512]{2,1,0:T(8,128)}, f32[64,3584]{1,0:T(8,128)}) custom-call(bf16[512,512]{1,0:T(8,128)(2,1)} %bitcast.6, bf16[512,64]{1,0:T(8,128)(2,1)} %bitcast.7, bf16[512,64]{1,0:T(8,128)(2,1)} %bitcast.8, bf16[512,64]{1,0:T(8,128)(2,1)} %bitcast.9, s32[8,8]{1,0:T(8,128)} %cols_ref.1, s32[8,8]{1,0:T(8,128)} %mask_ref.1, s32[8]{0:T(128)} %one_ref.1, ...), custom_call_target="tpu_custom_call" | custom-call | tf_op jit(solution)/shard_map/pallas_call | solution.py:801
  61.7 7.1 %shard_map.96 = (f32[512,3584]{1,0:T(8,128)}, f32[64,3584]{1,0:T(8,128)}) custom-call(f32[7,512,512]{2,1,0:T(8,128)} %get-tuple-element.6.blocks, f32[64,3584]{1,0:T(8,128)} %get-tuple-element.7.level), custom_call_target="tpu_custom_call" | custom-call | tf_op jit(solution)/shard_map/pallas_call | solution.py:832

commit v4 on v3

--- a/solution.py
+++ b/solution.py
@@ -12,7 +12,7 @@
 LANES = 128
 MESH = pl.DeviceIdType.MESH
 VMEM_LIMIT = 60 * 1024 * 1024
-FUSED_LIMIT = 50 * 1024 * 1024
+FUSED_LIMIT = 52 * 1024 * 1024
 F32 = jnp.float32
 BF16 = jnp.bfloat16
 
@@ -383,7 +383,7 @@
 def whole_kernel(
     n, blocks, slots, aggs, groups, tile,
     a_ref, d_ref, t_ref, q_ref, cols_ref, mask_ref, one_ref, two_ref, out, two,
-    ag, dg, tg, cg, ad, sd, pro, ts, t2s, t2t, hot, ids, bd, wm, cf, term, mine, rx1, tx2, rx2,
+    ag, dg, tg, cg, ad, sd, pro, ts, t2s, t2t, hot, bd, wm, cf, term, mine, rx1, tx2, rx2,
     send_sem, recv_sem, out_sem, send1, recv1, send2, recv2,
 ):
     s, p = lax.axis_index("slab"), lax.axis_index("piece")
@@ -407,14 +407,18 @@
     for mate in [sibling] + mates:
         pl.semaphore_signal(barrier, inc=1, device_id=(s, mate), device_id_type=MESH)
 
+    line = lax.broadcasted_iota(jnp.int32, cg.shape[1:], 0)
+    spot = lax.broadcasted_iota(jnp.int32, cg.shape[1:], 1)
+    packed = jnp.zeros(cg.shape[1:], jnp.int32)
     for i in range(blocks):
+        column = jnp.zeros(cg.shape[1:], jnp.int32)
         for k in range(slots):
             code = jnp.where(mask_ref[i, k] != 0, cols_ref[i, k], -1)
-            ids[i * slots + k : i * slots + k + 1, :] = jnp.full((1, pair), code, jnp.int32)
-        at = blocks * slots + i
-        ids[at : at + 1, :] = jnp.full((1, pair), one_ref[i], jnp.int32)
-        ids[at + blocks : at + blocks + 1, :] = jnp.full((1, pair), two_ref[i], jnp.int32)
-    cg[s] = ids[...].astype(F32).astype(BF16)
+            column = jnp.where(line == k, code, column)
+        column = jnp.where(line == slots, one_ref[i], column)
+        column = jnp.where(line == slots + 1, two_ref[i], column)
+        packed = jnp.where(spot == i, column, packed)
+    cg[s] = packed.astype(F32).astype(BF16)
     tg[s] = jnp.concatenate([t_ref[...], q_ref[...]], axis=1)
     dg[s] = jnp.concatenate([d_ref[0 : rows // 2, :], d_ref[rows // 2 : rows, :]], axis=1)
     ag[s] = a_ref[...]
@@ -477,18 +481,18 @@
         @pl.when(valid(e))
         def _():
             u = s + e
-            names = cg[u, blocks * slots :, :].astype(F32)
+            names = cg[u].astype(F32)
             for b in range(blocks):
                 x = tg[u, b * tile : (b + 1) * tile, :].astype(F32)
                 turned = pltpu.roll(x, tile, 1)
                 two_t = jnp.where(lane == 0, turned, x)
                 one_t = jnp.where(lane == 0, x, turned)
-                g1 = names[b : b + 1, :]
+                g1 = jnp.broadcast_to(names[slots : slots + 1, b : b + 1], (1, pair))
                 for q in range(w // pair):
                     ts[u, b * tile : (b + 1) * tile, q * pair : (q + 1) * pair] = jnp.where(
                         lane_f + 2.0 * q == g1, one_t, 0.0
                     ).astype(BF16)
-                g2 = names[blocks + b : blocks + b + 1, :]
+                g2 = jnp.broadcast_to(names[slots + 1 : slots + 2, b : b + 1], (1, pair))
                 for q in range(gw // pair):
                     t2s[u, b * tile : (b + 1) * tile, q * pair : (q + 1) * pair] = jnp.where(
                         lane_f + 2.0 * q == g2, two_t, 0.0
@@ -501,12 +505,15 @@
         def _():
             u = s + e
             if h == 0:
-                codes = cg[u, 0 : blocks * slots, :].astype(F32)
-                at = lax.broadcasted_iota(jnp.int32, (blocks * slots, pair), 1) // tile
+                codes = cg[u].astype(F32)
+                at = lax.broadcasted_iota(jnp.int32, (slots, pair), 1) // tile
                 at = at.astype(F32)
-                for cp in range(3 * rows // pair):
-                    hit = jnp.where(codes == at + 2.0 * cp, 1.0, 0.0)
-                    hot[:, :, cp * pair : (cp + 1) * pair] = hit.reshape(blocks, slots, pair)
+                for i in range(blocks):
+                    code = jnp.broadcast_to(codes[0:slots, i : i + 1], (slots, pair))
+                    for cp in range(3 * rows // pair):
+                        hot[i, :, cp * pair : (cp + 1) * pair] = jnp.where(
+                            code == at + 2.0 * cp, 1.0, 0.0
+                        )
 
             def row(i, carry):
                 base = pl.multiple_of(i * tile, tile)
@@ -579,7 +586,7 @@
 
     def leave(f):
         return pltpu.make_async_copy(
-            cf.at[f + 3], out.at[f + 3], out_sem.at[f + 3]
+            cf.at[f + 3], out.at[s + f if n < 7 else f + 3], out_sem.at[f + 3]
         )
 
     def sum_over(f, sides):
@@ -720,44 +727,33 @@
                 send(way, step, which, lambda c: c.wait_send())
 
 
-def place_kernel(n, blocks, level, out, two, held, zero, in_sem, out_sem):
+def place_kernel(n, blocks, level, out, two, zero, sem, last):
     s = lax.axis_index("slab")
-    w = zero.shape[0]
-
-    def write(f, source):
-        return pltpu.make_async_copy(source, out.at[:, pl.ds((f + 3) * w, w)], out_sem.at[f + 3])
-
-    def read(f):
-        return pltpu.make_async_copy(blocks.at[f + 3], held.at[f + 3], in_sem.at[f + 3])
-
-    def either(f, inside, outside):
-        ok = (s + f >= 0) & (s + f < n)
-
-        @pl.when(ok)
-        def _():
-            inside()
-
-        if outside is not None:
-
-            @pl.when(jnp.logical_not(ok))
-            def _():
-                outside()
-
-    for f in range(-3, 4):
-        either(f, lambda: read(f).start(), None)
+    cut, w = zero.shape
+    parts = w // cut
+    other = pltpu.make_async_copy(level, two, last)
+    other.start()
     zero[...] = jnp.zeros_like(zero)
-    for f in range(-3, 4):
-        either(f, lambda: None, lambda: write(f, zero).start())
-
-    def onward(f):
-        read(f).wait()
-        write(f, held.at[f + 3]).start()
-
-    for f in range(-3, 4):
-        either(f, lambda: onward(f), None)
-    two[...] = level[...]
-    for f in range(-3, 4):
-        either(f, lambda: write(f, held.at[f + 3]).wait(), lambda: write(f, zero).wait())
+
+    def each(act):
+        for f in range(-3, 4):
+            ok = (s + f >= 0) & (s + f < n)
+            for q in range(parts):
+                to = out.at[pl.ds(q * cut, cut), pl.ds((f + 3) * w, w)]
+
+                @pl.when(ok)
+                def _(f=f, q=q, to=to):
+                    slab = s + f if n < 7 else f + 3
+                    have = blocks.at[slab, pl.ds(q * cut, cut)]
+                    act(pltpu.make_async_copy(have, to, sem.at[f + 3, q]))
+
+                @pl.when(jnp.logical_not(ok))
+                def _(f=f, q=q, to=to):
+                    act(pltpu.make_async_copy(zero, to, sem.at[f + 3, q]))
+
+    each(lambda c: c.start())
+    each(lambda c: c.wait())
+    other.wait()
 
 
 def at_once(
@@ -769,7 +765,8 @@
     n, groups = lax.axis_size("slab"), lax.axis_size("piece")
     rows, w, gw = blocks * tile, aggs * tile, groups * tile
     pair, chips, far = 2 * tile, groups // 2, min(3, n - 1)
-    names = blocks * slots + 2 * blocks
+    names = -(-(slots + 2) // 16) * 16
+    kept = min(n, 7)
     vmem = pl.BlockSpec(memory_space=pltpu.VMEM)
     smem = pl.BlockSpec(memory_space=pltpu.SMEM)
     dma = pltpu.SemaphoreType.DMA
@@ -777,7 +774,7 @@
         pltpu.VMEM((n, rows, slots * tile), BF16),
         pltpu.VMEM((n, rows // 2, pair), BF16),
         pltpu.VMEM((n, rows, pair), BF16),
-        pltpu.VMEM((n, names, pair), BF16),
+        pltpu.VMEM((n, names, LANES), BF16),
         pltpu.VMEM((5, rows, 3 * rows), BF16),
         pltpu.VMEM((rows, 3 * rows), BF16),
         pltpu.VMEM((5, rows, 3 * w), BF16),
@@ -785,7 +782,6 @@
         pltpu.VMEM((n, w, gw), BF16),
         pltpu.VMEM((gw, w), BF16),
         pltpu.VMEM((blocks, slots, 3 * rows), F32),
-        pltpu.VMEM((names, pair), jnp.int32),
         pltpu.VMEM((rows // 2, rows // 2), BF16),
         pltpu.VMEM((5, w, rows), BF16),
         pltpu.VMEM((7, w, w), F32),
@@ -796,12 +792,12 @@
         pltpu.VMEM((7, chips - 1, tile, gw), BF16),
     ]
     size = sum(x.dtype.itemsize * np.prod(x.shape) for x in scratch)
-    if size > FUSED_LIMIT:
+    if size > 0.92 * FUSED_LIMIT:
         return None
     held, level_two = pl.pallas_call(
         functools.partial(whole_kernel, n, blocks, slots, aggs, groups, tile),
         out_shape=(
-            jax.ShapeDtypeStruct((7, w, w), F32),
+            jax.ShapeDtypeStruct((kept, w, w), F32),
             jax.ShapeDtypeStruct((tile, 7 * gw), F32),
         ),
         in_specs=[vmem] * 4 + [smem] * 4,
@@ -817,7 +813,7 @@
             dma((7, chips - 1)),
         ],
         compiler_params=pltpu.CompilerParams(
-            collective_id=2, has_side_effects=True, vmem_limit_bytes=VMEM_LIMIT
+            collective_id=2, has_side_effects=True, vmem_limit_bytes=FUSED_LIMIT
         ),
     )(
         fine_tiles.reshape(rows, slots * tile),
@@ -835,15 +831,14 @@
             jax.ShapeDtypeStruct((w, 7 * w), F32),
             jax.ShapeDtypeStruct((tile, 7 * gw), F32),
         ),
-        in_specs=[pl.BlockSpec(memory_space=pl.ANY), vmem],
-        out_specs=(pl.BlockSpec(memory_space=pl.ANY), vmem),
+        in_specs=[pl.BlockSpec(memory_space=pl.ANY)] * 2,
+        out_specs=(pl.BlockSpec(memory_space=pl.ANY),) * 2,
         scratch_shapes=[
-            pltpu.VMEM((7, w, w), F32),
-            pltpu.VMEM((w, w), F32),
-            dma((7,)),
-            dma((7,)),
+            pltpu.VMEM((w // 4, w), F32),
+            dma((7, 4)),
+            dma(()),
         ],
-        compiler_params=pltpu.CompilerParams(vmem_limit_bytes=VMEM_LIMIT),
+        compiler_params=pltpu.CompilerParams(vmem_limit_bytes=4 * 1024 * 1024),
     )(held, level_two)
     return (coarse.reshape(aggs, tile, 7 * w), level_two.reshape(1, tile, 7 * gw))
 

time: 69.2 us -> 72 us (1.040)
  local copies, waits for them, and re-layouts: 0 us -> 8.61 us
  Pallas kernels: 68.2 us -> 62.2 us
    unnamed x0 -> x18, local copies, waits for them, and re-layouts: none -> 8.61 us
    pallas_call x1, Pallas kernels: 7.1 us -> 3.51 us  [at_once(): pl.pallas_call(functools.partial(place_kernel, n), out_shape=(jax.ShapeDt...]
    pallas_call x1, Pallas kernels: 61.1 us -> 58.7 us  [at_once(): pl.pallas_call(functools.partial(whole_kernel, n, blocks, slots, aggs, gr...]
where the time goes in v4:
time: 72 us; the launch traced here: 71.6 us
  Pallas kernels  62.2 us (86%)
  local copies, waits for them, and re-layouts  8.61 us (12%)
  between operations  0.83 us (1%)
    pallas_call x1, Pallas kernels, at_once(): pl.pallas_call(functools.partial(whole_kernel, n, blocks, slots, aggs, gr...  58.7 us
    unnamed x18, local copies, waits for them, and re-layouts  8.61 us
    pallas_call x1, Pallas kernels, at_once(): pl.pallas_call(functools.partial(place_kernel, n), out_shape=(jax.ShapeDt...  3.51 us

profile of v4, /device:TPU:0, one launch (start us, length us, event | category | flops | bytes accessed | tf_op | source)
XLA Modules:
  0.0 71.6 jit_solution(6451876383378436034)
XLA Ops:
  0.6 0.0 copy-start.1
  0.6 1.0 %copy-done.1 = bf16[8,64,512]{2,1,0:T(8,128)(2,1)S(1)} copy-done((bf16[8,64,512]{2,1,0:T(8,128)(2,1)S(1)}, bf16[8,64,512]{2,1,0:T(8,128)(2,1)}, u32[]{:S(2)}) %copy-start.1) | copy-done | bytes 524312
  1.7 0.0 copy-start.2
  1.7 0.9 %copy-done.2 = bf16[8,64,64]{2,1,0:T(8,128)(2,1)S(1)} copy-done((bf16[8,64,64]{2,1,0:T(8,128)(2,1)S(1)}, bf16[8,64,64]{2,1,0:T(8,128)(2,1)}, u32[]{:S(2)}) %copy-start.2) | copy-done | bytes 65560
  2.6 0.0 copy-start.3
  2.6 0.9 %copy-done.3 = bf16[8,64,64]{2,1,0:T(8,128)(2,1)S(1)} copy-done((bf16[8,64,64]{2,1,0:T(8,128)(2,1)S(1)}, bf16[8,64,64]{2,1,0:T(8,128)(2,1)}, u32[]{:S(2)}) %copy-start.3) | copy-done | bytes 65560
  3.5 0.0 copy-start.4
  3.5 0.9 %copy-done.4 = bf16[8,64,64]{2,1,0:T(8,128)(2,1)S(1)} copy-done((bf16[8,64,64]{2,1,0:T(8,128)(2,1)S(1)}, bf16[8,64,64]{2,1,0:T(8,128)(2,1)}, u32[]{:S(2)}) %copy-start.4) | copy-done | bytes 65560
  4.4 0.0 copy-start.5
  4.4 0.7 copy-done.5
  5.1 0.0 copy-start.6
  5.1 0.7 copy-done.6
  5.8 0.0 copy-start.7
  5.8 0.7 copy-done.7
  6.4 0.0 copy-start.8
  6.4 0.7 copy-done.8
  7.1 58.7 %shard_map.95 = (f32[4,512,512]{2,1,0:T(8,128)}, f32[64,3584]{1,0:T(8,128)S(1)}) custom-call(bf16[512,512]{1,0:T(8,128)(2,1)S(1)} %bitcast.6, bf16[512,64]{1,0:T(8,128)(2,1)S(1)} %bitcast.7, bf16[512,64]{1,0:T(8,128)(2,1)S(1)} %bitcast.8, bf16[512,64]{1,0:T(8,128)(2,1)S(1)} %bitcast.9, s32[8,8]{1,0:T(8,128)S(1)} %copy-done.5, s32[8,8]{1,0:T(8,128)S(1)} %copy-done.6, ...), custom_call_target="tpu_custom_call" | custom-call | tf_op jit(solution)/shard_map/pallas_call | solution.py:797
  65.8 0.0 copy-start
  65.8 2.2 %copy-done = f32[4,512,512]{2,1,0:T(8,128)S(1)} copy-done((f32[4,512,512]{2,1,0:T(8,128)S(1)}, f32[4,512,512]{2,1,0:T(8,128)}, u32[]{:S(2)}) %copy-start) | copy-done | bytes 4194328
  68.0 3.5 %shard_map.96 = (f32[512,3584]{1,0:T(8,128)}, f32[64,3584]{1,0:T(8,128)}) custom-call(f32[4,512,512]{2,1,0:T(8,128)S(1)} %copy-done, f32[64,3584]{1,0:T(8,128)S(1)} %get-tuple-element.7.level), custom_call_target="tpu_custom_call" | custom-call | tf_op jit(solution)/shard_map/pallas_call | solution.py:828
Async XLA Ops:
  0.6 1.0 %copy-start.1 = (bf16[8,64,512]{2,1,0:T(8,128)(2,1)S(1)}, bf16[8,64,512]{2,1,0:T(8,128)(2,1)}, u32[]{:S(2)}) copy-start(bf16[8,64,512]{2,1,0:T(8,128)(2,1)} %param.8) | copy-start | bytes 1572868
  1.7 0.9 %copy-start.2 = (bf16[8,64,64]{2,1,0:T(8,128)(2,1)S(1)}, bf16[8,64,64]{2,1,0:T(8,128)(2,1)}, u32[]{:S(2)}) copy-start(bf16[8,64,64]{2,1,0:T(8,128)(2,1)} %param.11) | copy-start | bytes 196612
  2.6 0.9 %copy-start.3 = (bf16[8,64,64]{2,1,0:T(8,128)(2,1)S(1)}, bf16[8,64,64]{2,1,0:T(8,128)(2,1)}, u32[]{:S(2)}) copy-start(bf16[8,64,64]{2,1,0:T(8,128)(2,1)} %param.12) | copy-start | bytes 196612
  3.5 0.9 %copy-start.4 = (bf16[8,64,64]{2,1,0:T(8,128)(2,1)S(1)}, bf16[8,64,64]{2,1,0:T(8,128)(2,1)}, u32[]{:S(2)}) copy-start(bf16[8,64,64]{2,1,0:T(8,128)(2,1)} %param.14) | copy-start | bytes 196612
  4.4 0.7 copy-start.5
  5.1 0.7 copy-start.6
  5.8 0.7 copy-start.7
  6.4 0.7 copy-start.8
  65.8 2.2 %copy-start = (f32[4,512,512]{2,1,0:T(8,128)S(1)}, f32[4,512,512]{2,1,0:T(8,128)}, u32[]{:S(2)}) copy-start(f32[4,512,512]{2,1,0:T(8,128)} %get-tuple-element.6.blocks) | copy-start | bytes 12582916

commit v5 on v4

--- a/solution.py
+++ b/solution.py
@@ -813,7 +813,7 @@
             dma((7, chips - 1)),
         ],
         compiler_params=pltpu.CompilerParams(
-            collective_id=2, has_side_effects=True, vmem_limit_bytes=FUSED_LIMIT
+            collective_id=2, has_side_effects=True, vmem_limit_bytes=VMEM_LIMIT
         ),
     )(
         fine_tiles.reshape(rows, slots * tile),

time: 72 us -> 68 us (0.944)
  local copies, waits for them, and re-layouts: 8.61 us -> 3.36 us
  Pallas kernels: 62.2 us -> 63.6 us
    unnamed x18 -> x4, local copies, waits for them, and re-layouts: 8.61 us -> 3.36 us
    pallas_call x1, Pallas kernels: 58.7 us -> 60.1 us  [at_once(): pl.pallas_call(functools.partial(whole_kernel, n, blocks, slots, aggs, gr...]
where the time goes in v5:
time: 68 us; the launch traced here: 67.8 us
  Pallas kernels  63.6 us (94%)
  local copies, waits for them, and re-layouts  3.36 us (5%)
  between operations  0.81 us (1%)
    pallas_call x1, Pallas kernels, at_once(): pl.pallas_call(functools.partial(whole_kernel, n, blocks, slots, aggs, gr...  60.1 us
    pallas_call x1, Pallas kernels, at_once(): pl.pallas_call(functools.partial(place_kernel, n), out_shape=(jax.ShapeDt...  3.51 us
    unnamed x4, local copies, waits for them, and re-layouts  3.36 us

profile of v5, /device:TPU:0, one launch (start us, length us, event | category | flops | bytes accessed | tf_op | source)
XLA Modules:
  0.0 67.8 jit_solution(12981641786819329412)
XLA Ops:
  0.6 60.1 %shard_map.95 = (f32[4,512,512]{2,1,0:T(8,128)}, f32[64,3584]{1,0:T(8,128)}) custom-call(bf16[512,512]{1,0:T(8,128)(2,1)} %bitcast.6, bf16[512,64]{1,0:T(8,128)(2,1)} %bitcast.7, bf16[512,64]{1,0:T(8,128)(2,1)} %bitcast.8, bf16[512,64]{1,0:T(8,128)(2,1)} %bitcast.9, s32[8,8]{1,0:T(8,128)} %cols_ref.1, s32[8,8]{1,0:T(8,128)} %mask_ref.1, s32[8]{0:T(128)} %one_ref.1, ...), custom_call_target="tpu_custom_call" | custom-call | tf_op jit(solution)/shard_map/pallas_call | solution.py:797
  60.8 0.0 copy-start
  60.8 2.2 %copy-done = f32[4,512,512]{2,1,0:T(8,128)S(1)} copy-done((f32[4,512,512]{2,1,0:T(8,128)S(1)}, f32[4,512,512]{2,1,0:T(8,128)}, u32[]{:S(2)}) %copy-start) | copy-done | bytes 4194328
  63.0 0.0 copy-start.1
  63.0 1.2 %copy-done.1 = f32[64,3584]{1,0:T(8,128)S(1)} copy-done((f32[64,3584]{1,0:T(8,128)S(1)}, f32[64,3584]{1,0:T(8,128)}, u32[]{:S(2)}) %copy-start.1) | copy-done | bytes 917528
  64.1 3.5 %shard_map.96 = (f32[512,3584]{1,0:T(8,128)}, f32[64,3584]{1,0:T(8,128)}) custom-call(f32[4,512,512]{2,1,0:T(8,128)S(1)} %copy-done, f32[64,3584]{1,0:T(8,128)S(1)} %copy-done.1), custom_call_target="tpu_custom_call" | custom-call | tf_op jit(solution)/shard_map/pallas_call | solution.py:828
Async XLA Ops:
  60.8 2.2 %copy-start = (f32[4,512,512]{2,1,0:T(8,128)S(1)}, f32[4,512,512]{2,1,0:T(8,128)}, u32[]{:S(2)}) copy-start(f32[4,512,512]{2,1,0:T(8,128)} %get-tuple-element.6.blocks) | copy-start | bytes 12582916
  63.0 1.2 %copy-start.1 = (f32[64,3584]{1,0:T(8,128)S(1)}, f32[64,3584]{1,0:T(8,128)}, u32[]{:S(2)}) copy-start(f32[64,3584]{1,0:T(8,128)} %get-tuple-element.7.level) | copy-start | bytes 2752516
